TPU v7x, 32 devices: a whole 2x2x4 slice. The times are simulated.
32 devices in a mesh: section: 2 (over core), dp: 4 (over y, x), seq: 4 (over z).
Axes of the slice: x: 2, y: 2, z: 4, core: 2. Of those that a mesh axis runs over, the one named last changes fastest.
Arguments:
- layer_input: bfloat16 [2, 4, 1024, 768], P(None, 'dp', 'seq'), may hold values from -6 to 6
- out_cot: bfloat16 [2, 4, 1024, 768], P(None, 'dp', 'seq'), may hold values from -6 to 6
- doc_lengths: int32 [2, 4, 3], P(None, 'dp'), may hold values from 1 to 769, 1024 in all within a row
- norm_gains: bfloat16 [2, 2, 768], P('section'), may hold values from 0.5 to 1.5
- biases: bfloat16 [2, 4, 768], P('section'), may hold values from -1.796875 to 1.796875
- in_weight: bfloat16 [2, 768, 2304], P('section'), may hold values from -0.21875 to 0.21875
- mix_vecs: bfloat16 [2, 5, 2304], P('section'), may hold values from -3 to 3
- filt_first: bfloat16 [2, 33, 64], P('section'), may hold values from -1.5 to 1.5
- filt_inner_bias: bfloat16 [2, 2, 64], P('section'), may hold values from -3 to 3
- filt_second: bfloat16 [2, 64, 64], P('section'), may hold values from -1 to 1
- filt_last: bfloat16 [2, 64, 768], P('section'), may hold values from -0.059814453 to 0.059814453
- filt_skip: bfloat16 [2, 1, 768], P('section'), may hold values from -3 to 3
- out_weight: bfloat16 [2, 768, 768], P('section'), may hold values from -0.21875 to 0.21875
- up_weight: bfloat16 [2, 768, 3072], P('section'), may hold values from -0.21875 to 0.21875
- up_bias: bfloat16 [2, 1, 3072], P('section'), may hold values from -1.796875 to 1.796875
- down_weight: bfloat16 [2, 3072, 768], P('section'), may hold values from -0.109375 to 0.109375
Outputs:
- layer_output: float32 [2, 2, 4, 1024, 768], P('section', None, 'dp', 'seq')
- input_grad: float32 [2, 2, 4, 1024, 768], P('section', None, 'dp', 'seq')
- norm_gains_grad: float32 [2, 2, 768], P('section', None, ('dp', 'seq'))
- biases_grad: float32 [2, 4, 768], P('section', None, ('dp', 'seq'))
- in_weight_grad: float32 [2, 768, 2304], P('section', None, ('dp', 'seq'))
- mix_vecs_grad: float32 [2, 5, 2304], P('section', None, ('dp', 'seq'))
- filt_first_grad: float32 [2, 33, 64], P('section')
- filt_inner_bias_grad: float32 [2, 2, 64], P('section')
- filt_second_grad: float32 [2, 64, 64], P('section')
- filt_last_grad: float32 [2, 64, 768], P('section', None, ('dp', 'seq'))
- filt_skip_grad: float32 [2, 1, 768], P('section', None, ('dp', 'seq'))
- out_weight_grad: float32 [2, 768, 768], P('section', None, ('dp', 'seq'))
- up_weight_grad: float32 [2, 768, 3072], P('section', None, ('dp', 'seq'))
- up_bias_grad: float32 [2, 1, 3072], P('section', None, ('dp', 'seq'))
- down_weight_grad: float32 [2, 3072, 768], P('section', None, ('dp', 'seq'))
- penalty: float32 [], replicated
Inputs may be any that keep to these rules, and one draw needn't show every extreme that they name: `doc_lengths`: each row's 3 lengths are positive and sum to 1024; one of them is exactly 769.
All inputs are finite; a program needn't handle non-finite values.
Results may differ from a plain program's by a relative error of at most 0.015.
Values may be sent and summed in bfloat16 or wider, within the bound.
No kernel may reach another device: no remote copies, remote signals or barrier semaphores. Data moves between devices by JAX's collectives and lax.ppermute only.
A program may use at most 384 MiB of HBM per device.

v0:
```python
import jax
import jax.numpy as jnp
from jax import lax
from jax.sharding import PartitionSpec as P

D = 768
EMB = 33
SEQ = 1024
LONG_LAG = 32


eps = 1e-05
highest = lax.Precision.HIGHEST


def from_behind(value, axis, steps):
    count = lax.axis_size(axis)
    first, last = (max(0, -steps), min(count, count - steps))
    return lax.ppermute(value, axis, [(source, source + steps) for source in range(first, last)])


def layer_norm(values, gain_vec, shift_vec):
    centre = jnp.mean(values, axis=-1, keepdims=True)
    centred = values - centre
    variance = jnp.mean(centred * centred, axis=-1, keepdims=True)
    return centred * lax.rsqrt(variance + eps) * gain_vec + shift_vec


def gelu_tanh(values):
    return jax.nn.gelu(values, approximate=True)


def add_up(first_val, second_val):
    return first_val + second_val


def position_table():
    positions = jnp.arange(SEQ, dtype=jnp.float32)
    band_count = (EMB - 1) // 2
    band_freq = 0.0001 + jnp.arange(band_count, dtype=jnp.float32) * (
        (band_count - 1 - 0.0001) / (band_count - 1)
    )
    angles = 2.0 * jnp.pi / SEQ * positions[:, None] * band_freq[None, :]
    return jnp.concatenate([(positions / SEQ)[:, None], jnp.cos(angles), jnp.sin(angles)], axis=1)


def decay_table(channels, offset):
    times = jnp.arange(SEQ, dtype=jnp.float32)[:, None] / SEQ
    chan_ids = (jnp.arange(channels, dtype=jnp.int32) + offset).astype(jnp.float32)
    rates = 3.0 + 12.0 * chan_ids / (D - 1)
    return jnp.exp(-times * rates[None, :])


def filter_taps(first_w, inner_b, second_w, last_w, decay_vals):
    pos_table = position_table()
    hidden = jnp.sin(jnp.dot(pos_table, first_w, precision=highest) + inner_b[0])
    hidden = jnp.sin(jnp.dot(hidden, second_w, precision=highest) + inner_b[1])
    return jnp.dot(hidden, last_w, precision=highest) * decay_vals


def doc_masks(lengths):
    doc_ends = jnp.cumsum(lengths, axis=-1)
    doc_starts = doc_ends - lengths
    positions = jnp.arange(SEQ, dtype=jnp.int32)
    inside = (positions >= doc_starts[..., None]) & (positions < doc_ends[..., None])
    own_start = jnp.sum(jnp.where(inside, doc_starts[..., None], 0), axis=-2)
    return (inside.astype(jnp.float32), positions - own_start)


def dft_tables():
    freq_ids = jnp.arange(SEQ + 1, dtype=jnp.int32)
    phase = freq_ids[:, None] * jnp.arange(SEQ, dtype=jnp.int32)[None, :] % (2 * SEQ)
    angles = phase.astype(jnp.float32) * (jnp.pi / SEQ)
    freq_weight = jnp.where((freq_ids == 0) | (freq_ids == SEQ), 1.0, 2.0) / (2.0 * SEQ)
    return (jnp.cos(angles), jnp.sin(angles), freq_weight)


def channel_mix(stream_vals, short_vals, filt_vals, mask_now, place_now, tables, decay_vals):
    first_w, inner_b, second_w, last_w, skip_vec = filt_vals
    length = stream_vals.shape[1]
    mixed_in = short_vals[3] + short_vals[0] * stream_vals
    for step_back in (1, 2):
        earlier = jnp.pad(stream_vals, ((0, 0), (step_back, 0), (0, 0), (0, 0)))[:, :length]
        mixed_in = (
            mixed_in
            + short_vals[step_back]
            * earlier
            * (place_now >= step_back).astype(jnp.float32)[:, :, None, None]
        )
    gate_out = mixed_in[:, :, 0]
    inner_gate = mixed_in[:, :, 1]
    value_part = mixed_in[:, :, 2]
    signal = value_part * inner_gate
    filt_now = filter_taps(first_w, inner_b, second_w, last_w, decay_vals)
    cosine, sine_tab, freq_weight = tables
    taps_re = jnp.dot(cosine, filt_now, precision=highest)
    taps_im = -jnp.dot(sine_tab, filt_now, precision=highest)
    pieces = mask_now[:, :, :, None] * signal[:, None]
    sig_re = jnp.einsum("fl,rdlc->rdfc", cosine, pieces, precision=highest)
    sig_im = -jnp.einsum("fl,rdlc->rdfc", sine_tab, pieces, precision=highest)
    prod_re = (taps_re * sig_re - taps_im * sig_im) * freq_weight[:, None]
    prod_im = (taps_re * sig_im + taps_im * sig_re) * freq_weight[:, None]
    spread = jnp.einsum("fl,rdfc->rdlc", cosine, prod_re, precision=highest) - jnp.einsum(
        "fl,rdfc->rdlc", sine_tab, prod_im, precision=highest
    )
    conv_out = jnp.sum(spread * mask_now[:, :, :, None], axis=1)
    return (conv_out + skip_vec * signal) * gate_out


def local(
    layer_input,
    out_cot,
    doc_lengths,
    norm_gains,
    biases,
    in_weight,
    mix_vecs,
    filt_first,
    filt_inner_bias,
    filt_second,
    filt_last,
    filt_skip,
    out_weight,
    up_weight,
    up_bias,
    down_weight,
):
    as_float = jnp.float32
    channels = D // lax.axis_size("seq")
    chan_start = lax.axis_index("seq") * channels
    first_section = lax.axis_index("section") == 0
    micro_count = layer_input.shape[0]
    row_count = layer_input.shape[1]
    shard_len = layer_input.shape[2]
    gain_vecs = norm_gains[0].astype(as_float)
    bias_vecs = biases[0].astype(as_float)
    weight_in = in_weight[0]
    vec_rows = mix_vecs[0]
    in_bias = vec_rows[0].astype(as_float)
    short_local = lax.dynamic_slice_in_dim(
        vec_rows[1:].reshape(4, 3, D), chan_start, channels, 2
    ).astype(as_float)
    filt_local = (
        filt_first[0].astype(as_float),
        filt_inner_bias[0].astype(as_float),
        filt_second[0].astype(as_float),
        lax.dynamic_slice_in_dim(filt_last[0], chan_start, channels, 1).astype(as_float),
        lax.dynamic_slice_in_dim(filt_skip[0, 0], chan_start, channels, 0).astype(as_float),
    )
    weight_out = out_weight[0]
    weight_up = up_weight[0]
    hidden_bias = up_bias[0, 0].astype(as_float)
    weight_down = down_weight[0]
    decay_vals = decay_table(channels, chan_start)
    tables = dft_tables()
    doc_mask, doc_place = doc_masks(doc_lengths)

    def forward_part(inputs, mask_now, place_now):
        normed = layer_norm(inputs, gain_vecs[0], bias_vecs[0]).astype(jnp.bfloat16)
        streams = (
            jnp.einsum("rtd,de->rte", normed, weight_in, preferred_element_type=as_float) + in_bias
        ).astype(jnp.bfloat16)
        by_channel = lax.all_to_all(
            streams.reshape(row_count, shard_len, 3, D),
            "seq",
            split_axis=3,
            concat_axis=1,
            tiled=True,
        )

        def local_mix(stream_vals, short_vals, filt_vals):
            return channel_mix(
                stream_vals, short_vals, filt_vals, mask_now, place_now, tables, decay_vals
            )

        mixed_out, mix_pull = jax.vjp(
            local_mix, by_channel.astype(as_float), short_local, filt_local
        )
        gated_tok = lax.all_to_all(
            mixed_out.astype(jnp.bfloat16), "seq", split_axis=1, concat_axis=2, tiled=True
        )
        residual = (
            inputs
            + jnp.einsum("rtd,de->rte", gated_tok, weight_out, preferred_element_type=as_float)
            + bias_vecs[1]
        )
        normed_two = layer_norm(residual, gain_vecs[1], bias_vecs[2]).astype(jnp.bfloat16)
        pre_act = (
            jnp.einsum("rtd,df->rtf", normed_two, weight_up, preferred_element_type=as_float)
            + hidden_bias
        )
        hidden = gelu_tanh(pre_act).astype(jnp.bfloat16)
        result = (
            residual
            + jnp.einsum("rtf,fd->rtd", hidden, weight_down, preferred_element_type=as_float)
            + bias_vecs[3]
        )
        return (
            result,
            (inputs, normed, mix_pull, gated_tok, residual, normed_two, pre_act, hidden),
        )

    recv_act = jnp.zeros((row_count, shard_len, D), as_float)
    layer_outs = []
    stored = []
    for tick in range(micro_count + 1):
        own_micro = min(tick, micro_count - 1)
        prev_micro = max(tick - 1, 0)
        fresh_in = layer_input[own_micro].astype(as_float) * float(tick < micro_count)
        inputs = jnp.where(first_section, fresh_in, recv_act)
        mask_now = jnp.where(first_section, doc_mask[own_micro], doc_mask[prev_micro])
        place_now = jnp.where(first_section, doc_place[own_micro], doc_place[prev_micro])
        result, kept_state = forward_part(inputs, mask_now, place_now)
        layer_outs.append(result)
        stored.append((inputs, mask_now, place_now))
        if tick < micro_count:
            recv_act = from_behind(result, "section", 1)
    recv_grad = jnp.zeros((row_count, shard_len, D), as_float)
    input_grads = []
    summed = None
    narrow_total = None
    for back_tick in range(micro_count + 1):
        fwd_tick = micro_count - back_tick
        cot_micro = max(fwd_tick - 1, 0)
        live_flag = jnp.where(first_section, float(back_tick >= 1), float(back_tick < micro_count))
        grad_out = (
            jnp.where(first_section, recv_grad, out_cot[cot_micro].astype(as_float)) * live_flag
        )
        kept_state = forward_part(stored[fwd_tick][0], stored[fwd_tick][1], stored[fwd_tick][2])[1]
        (
            backward_inputs,
            backward_normed,
            backward_mix_pull,
            backward_gated_tok,
            backward_residual,
            backward_normed_two,
            backward_pre_act,
            backward_hidden,
        ) = kept_state
        grad_mlp = grad_out.astype(jnp.bfloat16)
        d_down = jnp.einsum(
            "rtf,rtd->fd", backward_hidden, grad_mlp, preferred_element_type=as_float
        )
        d_down_bias = jnp.sum(grad_mlp.astype(as_float), axis=(0, 1))
        d_hidden = jnp.einsum("rtd,fd->rtf", grad_mlp, weight_down, preferred_element_type=as_float)
        d_pre = jax.vjp(gelu_tanh, backward_pre_act)[1](d_hidden)[0].astype(jnp.bfloat16)
        d_up = jnp.einsum(
            "rtd,rtf->df", backward_normed_two, d_pre, preferred_element_type=as_float
        )
        d_up_bias = jnp.sum(d_pre.astype(as_float), axis=(0, 1))
        d_normed_two = jnp.einsum("rtf,df->rtd", d_pre, weight_up, preferred_element_type=as_float)
        norm_pull_two = jax.vjp(layer_norm, backward_residual, gain_vecs[1], bias_vecs[2])[1]
        d_resid_norm, d_gain_two, d_shift_two = norm_pull_two(d_normed_two)
        d_residual = grad_out + d_resid_norm
        grad_branch = d_residual.astype(jnp.bfloat16)
        d_out = jnp.einsum(
            "rtd,rte->de", backward_gated_tok, grad_branch, preferred_element_type=as_float
        )
        d_out_bias = jnp.sum(grad_branch.astype(as_float), axis=(0, 1))
        d_gated = jnp.einsum(
            "rte,de->rtd", grad_branch, weight_out, preferred_element_type=as_float
        ).astype(jnp.bfloat16)
        d_mixed = lax.all_to_all(d_gated, "seq", split_axis=2, concat_axis=1, tiled=True)
        d_stream_ch, d_short, d_filt = backward_mix_pull(d_mixed.astype(as_float))
        d_streams = lax.all_to_all(
            d_stream_ch.astype(jnp.bfloat16), "seq", split_axis=1, concat_axis=3, tiled=True
        ).reshape(row_count, shard_len, 3 * D)
        d_in = jnp.einsum(
            "rtd,rte->de", backward_normed, d_streams, preferred_element_type=as_float
        )
        d_in_bias = jnp.sum(d_streams.astype(as_float), axis=(0, 1))
        d_normed = jnp.einsum("rte,de->rtd", d_streams, weight_in, preferred_element_type=as_float)
        norm_pull_one = jax.vjp(layer_norm, backward_inputs, gain_vecs[0], bias_vecs[0])[1]
        d_input_norm, d_gain_one, d_shift_one = norm_pull_one(d_normed)
        d_inputs = d_residual + d_input_norm
        short_full = lax.dynamic_update_slice_in_dim(
            jnp.zeros((4, 3, D), as_float), d_short, chan_start, 2
        ).reshape(4, 3 * D)
        d_mix = jnp.concatenate([d_in_bias[None], short_full], axis=0)
        d_last = lax.dynamic_update_slice_in_dim(
            jnp.zeros((d_filt[3].shape[0], D), as_float), d_filt[3], chan_start, 1
        )
        d_skip = lax.dynamic_update_slice_in_dim(
            jnp.zeros((D,), as_float), d_filt[4], chan_start, 0
        )
        wide = (
            jnp.stack([d_gain_one, d_gain_two])[None],
            jnp.stack([d_shift_one, d_out_bias, d_shift_two, d_down_bias])[None],
            d_in[None],
            d_mix[None],
            d_last[None],
            d_skip[None, None],
            d_out[None],
            d_up[None],
            d_up_bias[None, None],
            d_down[None],
        )
        narrow = (d_filt[0], d_filt[1], d_filt[2])
        d_inputs, wide, narrow = (d_inputs, wide, narrow)
        input_grads.append(d_inputs)
        narrow_total = (
            narrow if narrow_total is None else jax.tree.map(add_up, narrow_total, narrow)
        )
        summed = wide if summed is None else jax.tree.map(add_up, summed, wide)
        if back_tick < micro_count:
            recv_grad = from_behind(d_inputs, "section", -1)
    summed = (
        lax.psum_scatter(summed[0], ("dp", "seq"), scatter_dimension=2, tiled=True),
        lax.psum_scatter(summed[1], ("dp", "seq"), scatter_dimension=2, tiled=True),
        lax.psum_scatter(summed[2], ("dp", "seq"), scatter_dimension=2, tiled=True),
        lax.psum_scatter(summed[3], ("dp", "seq"), scatter_dimension=2, tiled=True),
        lax.psum_scatter(summed[4], ("dp", "seq"), scatter_dimension=2, tiled=True),
        lax.psum_scatter(summed[5], ("dp", "seq"), scatter_dimension=2, tiled=True),
        lax.psum_scatter(summed[6], ("dp", "seq"), scatter_dimension=2, tiled=True),
        lax.psum_scatter(summed[7], ("dp", "seq"), scatter_dimension=2, tiled=True),
        lax.psum_scatter(summed[8], ("dp", "seq"), scatter_dimension=2, tiled=True),
        lax.psum_scatter(summed[9], ("dp", "seq"), scatter_dimension=2, tiled=True),
    )
    filt_sums = lax.psum((narrow_total[0], narrow_total[1], narrow_total[2]), ("dp", "seq"))
    filt_vals = filter_taps(filt_local[0], filt_local[1], filt_local[2], filt_local[3], decay_vals)
    energy = filt_vals * filt_vals
    tail_share = jnp.sum(jnp.sum(energy[LONG_LAG:], axis=0) / (jnp.sum(energy, axis=0) + 1e-06))
    layer_weight = 1.0 + 3.0 * lax.axis_index("section").astype(as_float)
    penalty = lax.psum(tail_share * layer_weight, ("section", "seq")) / channels
    out_stack = jnp.stack(
        [
            jnp.where(first_section, layer_outs[micro_pos], layer_outs[micro_pos + 1])
            for micro_pos in range(micro_count)
        ]
    )[None]
    grad_stack = jnp.stack(
        [
            jnp.where(
                first_section,
                input_grads[micro_count - micro_pos],
                input_grads[micro_count - 1 - micro_pos],
            )
            for micro_pos in range(micro_count)
        ]
    )[None]
    return (
        out_stack,
        grad_stack,
        summed[0],
        summed[1],
        summed[2],
        summed[3],
        filt_sums[0][None],
        filt_sums[1][None],
        filt_sums[2][None],
        summed[4],
        summed[5],
        summed[6],
        summed[7],
        summed[8],
        summed[9],
        penalty,
    )


def solution(mesh):
    return jax.shard_map(
        local,
        mesh=mesh,
        in_specs=(
            P(None, "dp", "seq", None),
            P(None, "dp", "seq", None),
            P(None, "dp", None),
            P("section", None, None),
            P("section", None, None),
            P("section", None, None),
            P("section", None, None),
            P("section", None, None),
            P("section", None, None),
            P("section", None, None),
            P("section", None, None),
            P("section", None, None),
            P("section", None, None),
            P("section", None, None),
            P("section", None, None),
            P("section", None, None),
        ),
        out_specs=(
            P("section", None, "dp", "seq", None),
            P("section", None, "dp", "seq", None),
            P("section", None, ("dp", "seq")),
            P("section", None, ("dp", "seq")),
            P("section", None, ("dp", "seq")),
            P("section", None, ("dp", "seq")),
            P("section", None, None),
            P("section", None, None),
            P("section", None, None),
            P("section", None, ("dp", "seq")),
            P("section", None, ("dp", "seq")),
            P("section", None, ("dp", "seq")),
            P("section", None, ("dp", "seq")),
            P("section", None, ("dp", "seq")),
            P("section", None, ("dp", "seq")),
            P(),
        ),
        check_vma=False,
    )
```

profile of v0, /device:TPU:0, one launch (start us, length us, event | category | flops | bytes accessed | tf_op | source)
XLA Modules:
  0.0 3076.8 jit_solution(7846494949525973960)
XLA Ops:
  55.3 21.2 fusion.287
  76.5 21.5 convolution_negate_fusion
  102.6 29.2 fusion.120
  131.9 29.5 fusion.105
  161.4 26.5 fusion.47
  187.9 26.7 fusion.260
  284.0 35.2 %all-to-all-done.2 = bf16[1,256,3,768]{1,2,0,3:T(4,128)(2,1)} async-done(((bf16[1,256,3,768]{1,2,0,3:T(4,128)(2,1)}), bf16[1,256,3,768]{1,2,0,3:T(4,128)(2,1)}, u32[]{:S(2)}, u32[]{:S(2)}) %all-to-all-start.2) | async-done | bytes 1179680 | tf_op jit(solution)/shard_map/all_to_all | solution.py:163
  323.8 29.0 fusion.125
  352.9 29.5 fusion.110
  382.4 26.5 fusion.43
  408.9 26.7 fusion.259
  496.4 40.4 %all_to_all.85 = bf16[1,256,3,768]{1,2,0,3:T(4,128)(2,1)S(1)} all-to-all(bf16[1,256,3,768]{1,2,0,3:T(4,128)(2,1)S(1)} %copy.289), channel_id=1, replica_groups=mesh['section'=2,'dp'=4,'seq'=4] {'seq'}, dimensions={3} | all-to-all | bytes 2359296 | tf_op jit(solution)/shard_map/all_to_all | solution.py:163
  540.1 29.0 fusion.130
  569.2 29.5 fusion.115
  598.7 26.5 fusion.39
  625.2 26.7 fusion.258
  745.8 29.1 fusion.61
  774.9 29.8 fusion.37
  804.7 27.3 fusion.35
  832.0 26.3 fusion.257
  870.2 50.4 %all_to_all.87 = bf16[1,1024,3,192]{3,2,0,1:T(4,128)(2,1)} all-to-all(bf16[1,1024,3,192]{3,2,0,1:T(4,128)(2,1)} %copy.299), channel_id=1, replica_groups=mesh['section'=2,'dp'=4,'seq'=4] {'seq'}, dimensions={1} | all-to-all | bytes 2359296 | tf_op jit(solution)/shard_map/all_to_all | solution.py:265
  957.3 16.4 all_to_all.88
  985.7 29.1 fusion.57
  1014.8 29.8 fusion.33
  1044.7 27.1 fusion.31
  1071.8 26.5 fusion.256
  1110.3 52.4 %all_to_all.89 = bf16[1,1024,3,192]{3,2,0,1:T(4,128)(2,1)} all-to-all(bf16[1,1024,3,192]{3,2,0,1:T(4,128)(2,1)} %copy.306), channel_id=1, replica_groups=mesh['section'=2,'dp'=4,'seq'=4] {'seq'}, dimensions={1} | all-to-all | bytes 2359296 | tf_op jit(solution)/shard_map/all_to_all | solution.py:265
  1268.6 30.6 fusion.29
  1299.2 42.1 %fusion.156 = (f32[1025,192]{0,1:T(8,128)}, f32[1025,192]{0,1:T(8,128)}, f32[1025,192]{0,1:T(8,128)}, f32[1025,192]{0,1:T(8,128)}, f32[1025,192]{0,1:T(8,128)}, ...) fusion(f32[1,3,1025,192]{2,3,1,0:T(8,128)S(1)} %copy-done.53, ...), kind=kOutput, calls=%fused_computation.155 | convolution fusion | flops 7287241216 | bytes 38588420 | tf_op jit(solution)/shard_map/transpose(jvp(fl,rdfc->rdlc))/dot_general | solution.py:103
  1341.4 30.1 fusion.27
  1371.5 26.3 fusion.255
  1500.9 20.8 copy.326
  1534.4 20.7 copy.325
  1585.0 16.6 copy.316
  1604.5 16.2 psum.31
  1634.4 22.0 fusion.280
  1656.5 19.6 fusion.366
  1679.9 22.0 fusion.282
  1701.9 19.6 fusion.360
  1726.4 22.0 fusion.284
  1748.4 19.4 fusion.354
  1784.1 76.6 %all-reduce.43 = (f32[1,33,64]{2,1,0:T(8,128)}, f32[1,2,64]{2,1,0:T(2,128)}, f32[1,64,64]{2,1,0:T(8,128)}) all-reduce(f32[1,33,64]{2,1,0:T(8,128)} %fusion.436, f32[1,2,64]{2,1,0:T(2,128)} %add_bitcast_fusion.4, f32[1,64,64]{2,1,0:T(8,128)} %fusion.435), channel_id=1, replica_groups=mesh['section'=2,'dp'=4,'seq'=4] {'dp','seq'}, use_global_device_ids=true, to_apply=%region_81.82 | all-reduce | flops 6336 | bytes 50688 | tf_op jit(solution)/shard_map/psum | solution.py:319
  1870.5 81.6 %reduce-scatter.21.cloned.1.call-done = f32[48,4]{1,0:T(8,128)} async-done(((f32[768,4]{1,0:T(8,128)}), f32[48,4]{1,0:T(8,128)}) %reduce-scatter.21.cloned.1.call-update) | async-done | bytes 784
  1953.5 127.4 %reduce-scatter.23.cloned.1.call-done = f32[144,5]{1,0:T(8,128)} async-done(((f32[2304,5]{1,0:T(8,128)}), f32[144,5]{1,0:T(8,128)}) %reduce-scatter.23.cloned.1.call-update) | async-done | bytes 2896
  2082.5 285.2 %all-reduce.51.cloned.1.call-done = f32[1,3072,768]{1,0,2:T(1,128)} async-done(((f32[1,3072,768]{1,0,2:T(1,128)}), f32[1,3072,768]{1,0,2:T(1,128)}) %all-reduce.51.cloned.1.call-update) | async-done | bytes 9437200
  2369.7 284.8 %all-reduce.49.cloned.1.call-done = f32[1,768,3072]{1,0,2:T(1,128)} async-done(((f32[1,768,3072]{1,0,2:T(1,128)}), f32[1,768,3072]{1,0,2:T(1,128)}) %all-reduce.49.cloned.1.call-update) | async-done | bytes 9437200
  2656.9 285.6 %all-reduce.53.cloned.1.call-done = (f32[1,768,2304]{1,0,2:T(1,128)}, f32[1,768,768]{1,0,2:T(1,128)}) async-done(((f32[1,768,2304]{1,0,2:T(1,128)}, f32[1,768,768]{1,0,2:T(1,128)}), (f32[1,768,2304]{1,0,2:T(1,128)}, f32[1,768,768]{1,0,2:T(1,128)})) %all-reduce.53.cloned.1.call-update) | async-done | bytes 9437200
  2946.2 122.6 %reduce-scatter.17.cloned.1.call-done = f32[1,64,48]{1,0,2:T(1,128)} async-done(((f32[1,64,768]{1,0,2:T(1,128)}), f32[1,64,48]{1,0,2:T(1,128)}) %reduce-scatter.17.cloned.1.call-update) | async-done | bytes 12304 | tf_op jit(solution)/shard_map/reduce_scatter | solution.py:312
  (895 shorter events, 665.0 us)
Async XLA Ops:
  12.6 476.4 %copy-start.122 = (f32[768]{0:T(1024)}, f32[768]{0:T(1024)S(1)}, u32[]{:S(2)}) copy-start(f32[768]{0:T(1024)S(1)} %get-tuple-element.170) | copy-start | bytes 9220
  12.6 681.0 %copy-start.124 = (f32[768]{0:T(1024)}, f32[768]{0:T(1024)S(1)}, u32[]{:S(2)}) copy-start(f32[768]{0:T(1024)S(1)} %get-tuple-element.167) | copy-start | bytes 9220
  21.6 76.3 %all-to-all-start = ((bf16[1,256,3,768]{1,2,0,3:T(4,128)(2,1)}), bf16[1,256,3,768]{1,2,0,3:T(4,128)(2,1)}, u32[]{:S(2)}, u32[]{:S(2)}) async-start(bf16[1,256,3,768]{1,2,0,3:T(4,128)(2,1)} %copy.275), calls=%async_computation | async-start | bytes 3145728 | tf_op jit(solution)/shard_map/all_to_all | solution.py:163
  102.4 112.2 %copy-start.1 = (f32[1,1024,3,192]{1,3,2,0:T(8,128)}, f32[1,1024,3,192]{1,3,2,0:T(8,128)S(1)}, u32[]{:S(2)}) copy-start(f32[1,1024,3,192]{1,3,2,0:T(8,128)S(1)} %multiply_add_fusion.2) | copy-start | bytes 7077892
  131.8 56.1 %copy-start.52 = (f32[1,3,1025,192]{2,3,1,0:T(8,128)}, f32[1,3,1025,192]{2,3,1,0:T(8,128)S(1)}, u32[]{:S(2)}) copy-start(f32[1,3,1025,192]{2,3,1,0:T(8,128)S(1)} %fusion.120) | copy-start | bytes 7084804
  131.8 29.5 copy-start.143
  131.9 29.5 copy-start.241
  131.9 29.5 copy-start.247
  228.6 16.3 all-to-all-start.1
  263.9 3.2 collective-permute-start
  276.8 42.4 %all-to-all-start.2 = ((bf16[1,256,3,768]{1,2,0,3:T(4,128)(2,1)}), bf16[1,256,3,768]{1,2,0,3:T(4,128)(2,1)}, u32[]{:S(2)}, u32[]{:S(2)}) async-start(bf16[1,256,3,768]{1,2,0,3:T(4,128)(2,1)} %copy.282), calls=%async_computation.2 | async-start | bytes 3145728 | tf_op jit(solution)/shard_map/all_to_all | solution.py:163
  323.7 112.0 %copy-start.3 = (f32[1,1024,3,192]{1,3,2,0:T(8,128)}, f32[1,1024,3,192]{1,3,2,0:T(8,128)S(1)}, u32[]{:S(2)}) copy-start(f32[1,1024,3,192]{1,3,2,0:T(8,128)S(1)} %multiply_add_fusion.1) | copy-start | bytes 7077892
  352.9 56.1 %copy-start.56 = (f32[1,3,1025,192]{2,3,1,0:T(8,128)}, f32[1,3,1025,192]{2,3,1,0:T(8,128)S(1)}, u32[]{:S(2)}) copy-start(f32[1,3,1025,192]{2,3,1,0:T(8,128)S(1)} %fusion.125) | copy-start | bytes 7084804
  484.7 3.2 collective-permute-start.1
  539.9 112.0 %copy-start.6 = (f32[1,1024,3,192]{1,3,2,0:T(8,128)}, f32[1,1024,3,192]{1,3,2,0:T(8,128)S(1)}, u32[]{:S(2)}) copy-start(f32[1,1024,3,192]{1,3,2,0:T(8,128)S(1)} %multiply_add_fusion) | copy-start | bytes 7077892
  569.1 56.1 %copy-start.60 = (f32[1,3,1025,192]{2,3,1,0:T(8,128)}, f32[1,3,1025,192]{2,3,1,0:T(8,128)S(1)}, u32[]{:S(2)}) copy-start(f32[1,3,1025,192]{2,3,1,0:T(8,128)S(1)} %fusion.130) | copy-start | bytes 7084804
  665.3 15.7 all-to-all-start.5
  774.8 57.1 %copy-start.62 = (f32[3,192,1025]{2,1,0:T(8,128)}, f32[3,192,1025]{2,1,0:T(8,128)S(1)}, u32[]{:S(2)}) copy-start(f32[3,192,1025]{2,1,0:T(8,128)S(1)} %fusion.61) | copy-start | bytes 7084804
  774.9 29.8 copy-start.146
  774.9 29.8 copy-start.244
  774.9 29.8 copy-start.250
  930.8 4.4 collective-permute-start.2
  1014.8 57.0 %copy-start.64 = (f32[3,192,1025]{2,1,0:T(8,128)}, f32[3,192,1025]{2,1,0:T(8,128)S(1)}, u32[]{:S(2)}) copy-start(f32[3,192,1025]{2,1,0:T(8,128)S(1)} %fusion.57) | copy-start | bytes 7084804
  1014.8 29.9 copy-start.147
  1014.8 29.9 copy-start.245
  1014.8 29.9 copy-start.251
  1173.8 4.5 collective-permute-start.3
  1207.2 49.3 %all-to-all-start.10 = ((bf16[4,2,24576]{2,1,0:T(2,128)(2,1)}), bf16[4,2,24576]{2,1,0:T(2,128)(2,1)}, u32[]{:S(2)}, u32[]{:S(2)}) async-start(bf16[4,2,24576]{2,1,0:T(2,128)(2,1)} %reshape.2786), calls=%async_computation.10 | async-start | bytes 786432 | tf_op jit(solution)/shard_map/all_to_all | solution.py:263
  1268.5 30.7 copy-start.53
  1268.6 30.6 copy-start.55
  1268.6 30.6 copy-start.57
  1268.6 30.6 copy-start.59
  1268.6 30.6 copy-start.148
  1299.2 42.2 %copy-start.246 = (f32[1025,192]{0,1:T(8,128)S(1)}, f32[1025,192]{0,1:T(8,128)}, u32[]{:S(2)}) copy-start(f32[1025,192]{0,1:T(8,128)} %fusion.287) | copy-start | bytes 2361604
  1341.4 30.1 copy-start.66
  1341.4 30.1 copy-start.67
  1341.4 30.1 copy-start.252
  1409.8 52.8 %all-to-all-start.11 = ((bf16[1,1024,3,192]{3,2,0,1:T(4,128)(2,1)}), bf16[1,1024,3,192]{3,2,0,1:T(4,128)(2,1)}, u32[]{:S(2)}, u32[]{:S(2)}) async-start(bf16[1,1024,3,192]{3,2,0,1:T(4,128)(2,1)} %copy.313), calls=%async_computation.11 | async-start | bytes 4194304 | tf_op jit(solution)/shard_map/all_to_all | solution.py:265
  1415.0 217.8 %reduce-scatter.27.cloned.1.call-start = ((), (), s32[]{:S(2)}) async-start(), calls=%async_computation.23 | async-start | bytes 1671168
  1448.5 415.5 %reduce-scatter.25.cloned.1.call-start = ((), (), s32[]{:S(2)}) async-start(), calls=%async_computation.22 | async-start | bytes 417792
  1457.8 411.4 %reduce-scatter.19.cloned.1.call-start = ((), (), s32[]{:S(2)}) async-start(), calls=%async_computation.19 | async-start | bytes 417792
  1476.0 476.1 %reduce-scatter.21.cloned.1.call-start = ((), (), s32[]{:S(2)}) async-start(), calls=%async_computation.20 | async-start | bytes 417792
  1482.2 598.7 %reduce-scatter.23.cloned.1.call-start = ((), (), s32[]{:S(2)}) async-start(), calls=%async_computation.21 | async-start | bytes 1253376
  1487.2 880.5 %all-reduce.51.cloned.1.call-start = ((), (), s32[]{:S(2)}) async-start(), calls=%async_computation.25 | async-start | bytes 18874368
  1521.8 1132.8 %all-reduce.49.cloned.1.call-start = ((), (), s32[]{:S(2)}) async-start(), calls=%async_computation.24 | async-start | bytes 18874368
  1555.1 1387.4 %all-reduce.53.cloned.1.call-start = ((), (), s32[]{:S(2)}) async-start(), calls=%async_computation.26 | async-start | bytes 18874368
  1601.7 1467.2 %reduce-scatter.17.cloned.1.call-start = ((), (), s32[]{:S(2)}) async-start(), calls=%async_computation.18 | async-start | bytes 417792 | tf_op jit(solution)/shard_map/reduce_scatter | solution.py:312
  1778.4 87.6 %copy-start.233 = (f32[256]{0:T(256)S(1)}, f32[256]{0:T(256)}, u32[]{:S(2)}) copy-start(f32[256]{0:T(256)} %copy-done.232) | copy-start | bytes 3076
  (232 other events, 1639.7 us)
Sparse Core Ops, SparseCore 0:
  1448.6 126.3 reduce-scatter.26
  1579.7 120.5 reduce-scatter.24
  1706.2 120.4 reduce-scatter.18
  1831.8 120.3 reduce-scatter.20
  1957.5 123.4 reduce-scatter.22
  2088.0 279.6 all-reduce.50
  2374.8 279.6 all-reduce.48
  2662.0 280.4 all-reduce.52
  2948.4 120.3 reduce-scatter.16
where the time goes:
time: 3090 us; the launch traced here: 3080 us
  waiting for transfers between devices  1260 us (41%)
  matrix products  1020 us (33%)
  local copies, waits for them, and re-layouts  318 us (10%)
  blocking collectives  283 us (9%)
  other arithmetic  140 us (5%)
  starting transfers between devices  35.6 us (1%)
    unnamed x17, waiting for transfers between devices  1060 us
    dot_general x6, matrix products, channel_mix(): jnp.einsum('fl,rdfc->rdlc', cosine, prod_re, precision=highest)  180 us
    dot_general x6, matrix products, channel_mix(): sig_im = -jnp.einsum('fl,rdlc->rdfc', sine_tab, pieces, precision=highest)  172 us
    dot_general x6, matrix products, channel_mix(): jnp.einsum('fl,rdfc->rdlc', sine_tab, prod_im, precision=highest)  170 us
    dot_general x6, matrix products, channel_mix(): sig_re = jnp.einsum('fl,rdlc->rdfc', cosine, pieces, precision=highest)  167 us
    reduce_scatter x1, waiting for transfers between devices, local(): lax.psum_scatter(summed[4], ('dp', 'seq'), scatter_dimension=2, tiled=True)  123 us
    all_to_all x2, blocking collectives, local(): lax.all_to_all(d_stream_ch.astype(jnp.bfloat16), 'seq', split_axis=1, con...  103 us
    dot_general x4, matrix products, channel_mix(): taps_re = jnp.dot(cosine, filt_now, precision=highest)  87.2 us
  transfers between devices with their start and end apart: 19, of which 14 were waited for; matrix products, arithmetic and copies ran while one was open for 16% of the time, Pallas kernels for 0%

commit v1 on v0

v1 whole, which is shorter than its diff:
```python
import functools

import jax
import jax.numpy as jnp
import ml_dtypes
import numpy as np
from jax import lax
from jax.experimental import pallas as pl
from jax.experimental.pallas import tpu as pltpu
from jax.sharding import PartitionSpec as P

D = 768
FF = 3072
EMB = 33
FILT = 64
SEQ = 1024
NDOCS = 3
LONG_LAG = 32
BLK = 128
NB = SEQ // BLK
FREQ = 2 * BLK
PIECES = NB + NDOCS - 1
HALO = 16
TILE = 48
FF_TILE = 512

eps = 1e-05
highest = lax.Precision.HIGHEST
f32 = jnp.float32
bf16 = jnp.bfloat16
VMEM_LIMIT = 56 * 1024 * 1024


def split_table(table):
    high = table.astype(ml_dtypes.bfloat16)
    low = (table - high.astype(np.float64)).astype(ml_dtypes.bfloat16)
    return high, low


def ring_table(offsets):
    theta = 2.0 * np.pi * (np.arange(BLK) + 0.5) / FREQ
    angles = offsets[:, None] * theta[None, :]
    return np.concatenate([np.cos(angles), -np.sin(angles)], axis=1)


def block_tables():
    fwd = ring_table(np.arange(BLK, dtype=np.float64))
    fwd_hi, fwd_lo = split_table(fwd)
    inv_hi, inv_lo = split_table(fwd.T / BLK)
    window = ring_table(np.arange(FREQ, dtype=np.float64) - BLK)
    window[0] = 0.0
    return fwd_hi, fwd_lo, inv_hi, inv_lo, window.astype(np.float32)


def position_table():
    positions = np.arange(SEQ, dtype=np.float32)
    band_count = (EMB - 1) // 2
    band_freq = np.float32(0.0001) + np.arange(band_count, dtype=np.float32) * np.float32(
        (band_count - 1 - 0.0001) / (band_count - 1)
    )
    angles = np.float32(2.0 * np.pi / SEQ) * positions[:, None] * band_freq[None, :]
    return np.concatenate(
        [(positions / SEQ)[:, None], np.cos(angles), np.sin(angles)], axis=1
    ).T.astype(np.float32)


def dot(left, right, dims=((1,), (0,))):
    return lax.dot_general(left, right, (dims, ((), ())), preferred_element_type=f32)


NT = ((1,), (1,))
TN = ((0,), (0,))


def norm_stats(values):
    centre = jnp.mean(values, axis=-1, keepdims=True)
    centred = values - centre
    variance = jnp.mean(centred * centred, axis=-1, keepdims=True)
    scale = lax.rsqrt(variance + eps)
    return centred * scale, scale


def norm_back(grad, gain, unit, scale):
    scaled = grad * gain
    return scale * (
        scaled
        - jnp.mean(scaled, axis=-1, keepdims=True)
        - unit * jnp.mean(scaled * unit, axis=-1, keepdims=True)
    )


def col_sum(values):
    return jnp.sum(values, axis=0, keepdims=True)


def place_masks(sc, rows, shard_len):
    pos = sc[1] * shard_len + lax.broadcasted_iota(jnp.int32, (rows, 1), 0)
    starts = pos == sc[2]
    after = pos == sc[2] + 1
    for doc in range(1, NDOCS):
        starts = starts | (pos == sc[2 + doc])
        after = after | (pos == sc[2 + doc] + 1)
    one = jnp.where(starts, 0.0, 1.0)
    two = jnp.where(starts | after, 0.0, 1.0)
    return one, two


def shifted(stream_ext):
    ext = stream_ext.astype(f32)
    return (
        ext[HALO:],
        pltpu.roll(ext, 1, 0)[HALO:],
        pltpu.roll(ext, 2, 0)[HALO:],
    )


def mix_row(p_ref, which, stream):
    row = 6 + 3 * which + stream
    return p_ref[row : row + 1, :]


def short_conv(st_ref, p_ref, stream, masks):
    zero, one, two = shifted(st_ref[:, stream * D : (stream + 1) * D])
    return (
        mix_row(p_ref, 4, stream)
        + mix_row(p_ref, 1, stream) * zero
        + mix_row(p_ref, 2, stream) * (one * masks[0])
        + mix_row(p_ref, 3, stream) * (two * masks[1])
    )


def fetch(own_first, own, rcv, dst, sem):
    @pl.when(own_first)
    def _():
        pltpu.make_async_copy(own, dst, sem).start()

    @pl.when(jnp.logical_not(own_first))
    def _():
        pltpu.make_async_copy(rcv, dst, sem).start()


def rows_at(start, size):
    return pl.ds(pl.multiple_of(start, 16), size)


def fetch_in(own_first, own, rcv, weight, sems):
    def part(ref, stream):
        return ref.at[0, :, pl.ds(stream * D, D)]

    def dest(stream):
        return weight.at[:, pl.ds(stream * D, D)]

    for stream in range(3):
        fetch(own_first, part(own, stream), part(rcv, stream), dest(stream), sems.at[stream])

    def wait(stream):
        pltpu.make_async_copy(part(own, stream), dest(stream), sems.at[stream]).wait()

    return wait


SMEM = pl.BlockSpec(memory_space=pltpu.SMEM)
VMEM = pl.BlockSpec(memory_space=pltpu.VMEM)
ANY = pl.BlockSpec(memory_space=pl.ANY)


def run(body, outs, ins, specs, scratch, name, flops=0, bytes_accessed=0):
    return pl.pallas_call(
        body,
        out_shape=[jax.ShapeDtypeStruct(shape, dtype) for shape, dtype in outs],
        in_specs=specs,
        out_specs=[VMEM] * len(outs),
        scratch_shapes=scratch,
        compiler_params=pltpu.CompilerParams(vmem_limit_bytes=VMEM_LIMIT),
        cost_estimate=pl.CostEstimate(
            flops=flops, bytes_accessed=bytes_accessed, transcendentals=0
        ),
        name=name,
    )(*ins)


def in_part(block, shard_len, count):
    chan = D // count

    def body(sc, x_ref, halo_ref, p_ref, own, rcv, normed_ref, st_ref, *rest):
        outs = rest[:count]
        weight, sig_t, sems = rest[count:]
        wait = fetch_in(sc[0] == block, own, rcv, weight, sems)
        ext = jnp.concatenate([halo_ref[...].astype(f32), x_ref[...].astype(f32)], axis=0)
        unit, _ = norm_stats(ext)
        normed = (unit * p_ref[0:1, :] + p_ref[2:3, :]).astype(bf16)
        normed_ref[...] = normed[HALO:]
        for stream in range(3):
            wait(stream)
            cols = slice(stream * D, (stream + 1) * D)
            st_ref[:, cols] = (dot(normed, weight[:, cols]) + mix_row(p_ref, 0, stream)).astype(bf16)
        masks = place_masks(sc, shard_len, shard_len)
        signal = short_conv(st_ref, p_ref, 2, masks) * short_conv(st_ref, p_ref, 1, masks)
        sig_t[...] = signal.T.astype(bf16)
        for step in range(count):
            outs[step][...] = sig_t[rows_at((sc[1] ^ step) * chan, chan), :]

    def call(sc, x, halo, params, own, rcv):
        return run(
            body,
            [((shard_len, D), bf16), ((shard_len + HALO, 3 * D), bf16)]
            + [((chan, shard_len), bf16)] * count,
            (sc, x, halo, params, own, rcv),
            [SMEM, VMEM, VMEM, VMEM, ANY, ANY],
            [
                pltpu.VMEM((D, 3 * D), bf16),
                pltpu.VMEM((D, shard_len), bf16),
                pltpu.SemaphoreType.DMA((3,)),
            ],
            f"in_part_{block}",
            2 * shard_len * D * 3 * D,
            D * 3 * D * 2,
        )

    return call


def piece_scalars(sc):
    starts = [sc[2 + doc] for doc in range(NDOCS)] + [SEQ]
    lows, offsets = [], [0]
    for doc in range(NDOCS):
        low, high = starts[doc] // BLK, (starts[doc + 1] - 1) // BLK
        lows.append(low)
        offsets.append(offsets[-1] + high - low + 1)
    pieces = []
    for piece in range(PIECES):
        begin, stop, low, first, last = starts[0], starts[1], lows[0], offsets[0], offsets[1]
        for doc in range(1, NDOCS):
            here = piece >= offsets[doc]
            begin = jnp.where(here, starts[doc], begin)
            stop = jnp.where(here, starts[doc + 1], stop)
            low = jnp.where(here, lows[doc], low)
            first = jnp.where(here, offsets[doc], first)
            last = jnp.where(here, offsets[doc + 1], last)
        live = piece < offsets[NDOCS]
        blk = jnp.minimum(low + piece - first, NB - 1)
        begin = jnp.where(live, begin, 0)
        stop = jnp.where(live, stop, 0)
        first = jnp.where(live, first, piece + 1)
        last = jnp.where(live, last, piece)
        pieces.append((blk, begin, stop, first, last))
    return pieces


def piece_mask(piece):
    pos = piece[0] * BLK + lax.broadcasted_iota(jnp.int32, (1, BLK), 1)
    return (pos >= piece[1]) & (pos < piece[2])


def gather_blocks(sc, ins, blocks, per_shard):
    for step, ref in enumerate(ins):
        source = sc[1] ^ step
        for part in range(per_shard):
            blocks[source * per_shard + part] = ref[:, part * BLK : (part + 1) * BLK]


def to_freq(pieces, blocks, masked, freq, tables, chan):
    for index, piece in enumerate(pieces):
        keep = jnp.where(piece_mask(piece), 1.0, 0.0)
        masked[index * chan : (index + 1) * chan, :] = (
            blocks[piece[0]].astype(f32) * keep
        ).astype(bf16)
    values = masked[...]
    freq[...] = dot(values, tables[0][...]) + dot(values, tables[1][...])


def from_freq(pieces, freq, out_blocks, tables, chan):
    values = freq[...]
    high = values.astype(bf16)
    low = (values - high.astype(f32)).astype(bf16)
    back = dot(high, tables[2][...]) + dot(low, tables[2][...]) + dot(high, tables[3][...])
    for index, piece in enumerate(pieces):
        mine = back[index * chan : (index + 1) * chan, :]
        before = out_blocks[piece[0]]
        out_blocks[piece[0]] = jnp.where(piece_mask(piece), mine, before)


def scatter_blocks(sc, outs, out_blocks, per_shard):
    for step, ref in enumerate(outs):
        target = sc[1] ^ step
        for part in range(per_shard):
            ref[:, part * BLK : (part + 1) * BLK] = out_blocks[target * per_shard + part].astype(bf16)


def conv_part(block, shard_len, count):
    chan = D // count
    per_shard = shard_len // BLK
    tiles = chan // TILE

    def body(sc, filt, *rest):
        ins, tables, rest = rest[:count], rest[count : count + 4], rest[count + 4 :]
        outs, blocks = rest[:count], rest[count]
        masked, freq, total, out_blocks = rest[count + 1 :]
        gather_blocks(sc, ins, blocks, per_shard)
        pieces = piece_scalars(sc)
        to_freq(pieces, blocks, masked, freq, tables, chan)
        for index, piece in enumerate(pieces):
            for tile in range(tiles):

                def step(other, carry, index=index, piece=piece, tile=tile):
                    sum_re, sum_im = carry
                    rows = rows_at(other * chan + tile * TILE, TILE)
                    sig_re, sig_im = freq[rows, :BLK], freq[rows, BLK:]
                    lag = index - other
                    here = slice(tile * TILE, (tile + 1) * TILE)
                    fil_re, fil_im = filt[lag, here, :BLK], filt[lag, here, BLK:]
                    return (
                        sum_re + fil_re * sig_re - fil_im * sig_im,
                        sum_im + fil_re * sig_im + fil_im * sig_re,
                    )

                zero = jnp.zeros((TILE, BLK), f32)
                sum_re, sum_im = lax.fori_loop(piece[3], index + 1, step, (zero, zero))
                here = slice(index * chan + tile * TILE, index * chan + (tile + 1) * TILE)
                total[here, :BLK] = sum_re
                total[here, BLK:] = sum_im
        out_blocks[...] = jnp.zeros_like(out_blocks)
        from_freq(pieces, total, out_blocks, tables, chan)
        scatter_blocks(sc, outs, out_blocks, per_shard)

    def call(sc, filt, ins, tables):
        return run(
            body,
            [((chan, shard_len), bf16)] * count + [((NB, chan, BLK), bf16)],
            (sc, filt, *ins, *tables),
            [SMEM] + [VMEM] * (count + 5),
            [
                pltpu.VMEM((PIECES * chan, BLK), bf16),
                pltpu.VMEM((PIECES * chan, FREQ), f32),
                pltpu.VMEM((PIECES * chan, FREQ), f32),
                pltpu.VMEM((NB, chan, BLK), f32),
            ],
            f"conv_part_{block}",
            10 * PIECES * chan * BLK * FREQ,
            NB * chan * FREQ * 4,
        )

    return call


def conv_back(block, shard_len, count):
    chan = D // count
    per_shard = shard_len // BLK
    tiles = chan // TILE

    def body(sc, filt, blocks, *rest):
        ins, tables, rest = rest[:count], rest[count : count + 4], rest[count + 4 :]
        outs, d_filt = rest[:count], rest[count]
        d_blocks, masked, freq, d_freq, total, out_blocks = rest[count + 1 :]
        gather_blocks(sc, ins, d_blocks, per_shard)
        pieces = piece_scalars(sc)
        to_freq(pieces, blocks, masked, freq, tables, chan)
        to_freq(pieces, d_blocks, masked, d_freq, tables, chan)
        d_filt[...] = jnp.zeros_like(d_filt)
        for index, piece in enumerate(pieces):
            for tile in range(tiles):
                rows = slice(index * chan + tile * TILE, index * chan + (tile + 1) * TILE)
                here = slice(tile * TILE, (tile + 1) * TILE)

                def step(other, carry, index=index, here=here, rows=rows, tile=tile):
                    sum_re, sum_im = carry
                    sig_re, sig_im = freq[rows, :BLK], freq[rows, BLK:]
                    there = rows_at(other * chan + tile * TILE, TILE)
                    der_re, der_im = d_freq[there, :BLK], d_freq[there, BLK:]
                    lag = other - index
                    fil_re, fil_im = filt[lag, here, :BLK], filt[lag, here, BLK:]
                    d_filt[lag, here, :BLK] += sig_re * der_re + sig_im * der_im
                    d_filt[lag, here, BLK:] += sig_re * der_im - sig_im * der_re
                    return (
                        sum_re + fil_re * der_re + fil_im * der_im,
                        sum_im + fil_re * der_im - fil_im * der_re,
                    )

                zero = jnp.zeros((TILE, BLK), f32)
                sum_re, sum_im = lax.fori_loop(index, piece[4], step, (zero, zero))
                total[rows, :BLK] = sum_re
                total[rows, BLK:] = sum_im
        out_blocks[...] = jnp.zeros_like(out_blocks)
        from_freq(pieces, total, out_blocks, tables, chan)
        scatter_blocks(sc, outs, out_blocks, per_shard)

    def call(sc, filt, blocks, ins, tables):
        return run(
            body,
            [((chan, shard_len), bf16)] * count + [((NB, chan, FREQ), f32)],
            (sc, filt, blocks, *ins, *tables),
            [SMEM] + [VMEM] * (count + 6),
            [
                pltpu.VMEM((NB, chan, BLK), bf16),
                pltpu.VMEM((PIECES * chan, BLK), bf16),
                pltpu.VMEM((PIECES * chan, FREQ), f32),
                pltpu.VMEM((PIECES * chan, FREQ), f32),
                pltpu.VMEM((PIECES * chan, FREQ), f32),
                pltpu.VMEM((NB, chan, BLK), f32),
            ],
            f"conv_back_{block}",
            14 * PIECES * chan * BLK * FREQ,
            NB * chan * FREQ * 8,
        )

    return call


def token_major(sc, ins, turned, chan):
    for step, ref in enumerate(ins):
        turned[rows_at((sc[1] ^ step) * chan, chan), :] = ref[...]
    return turned[...].astype(f32).T


def weight_scratch():
    return [
        pltpu.VMEM((D, D), bf16),
        pltpu.VMEM((D, FF), bf16),
        pltpu.VMEM((FF, D), bf16),
        pltpu.SemaphoreType.DMA((1 + 2 * (FF // FF_TILE),)),
    ]


def fetch_mlp(own_first, pairs, dsts, sems, out_first):
    tiles = FF // FF_TILE
    (out_own, out_rcv), (up_own, up_rcv), (down_own, down_rcv) = pairs
    w_out, w_up, w_down = dsts

    def start_out():
        fetch(own_first, out_own.at[0], out_rcv.at[0], w_out, sems.at[0])

    def start_up(tile):
        cols = pl.ds(tile * FF_TILE, FF_TILE)
        fetch(
            own_first,
            up_own.at[0, :, cols],
            up_rcv.at[0, :, cols],
            w_up.at[:, cols],
            sems.at[1 + tile],
        )

    def start_down(tile):
        rows = pl.ds(tile * FF_TILE, FF_TILE)
        fetch(
            own_first,
            down_own.at[0, rows],
            down_rcv.at[0, rows],
            w_down.at[rows],
            sems.at[1 + tiles + tile],
        )

    if out_first:
        start_out()
    for tile in range(tiles):
        if out_first:
            start_up(tile)
            start_down(tile)
        else:
            start_down(tile)
            start_up(tile)
    if not out_first:
        start_out()

    def wait_out():
        pltpu.make_async_copy(out_own.at[0], w_out, sems.at[0]).wait()

    def wait_up(tile):
        cols = pl.ds(pl.multiple_of(tile * FF_TILE, FF_TILE), FF_TILE)
        pltpu.make_async_copy(up_own.at[0, :, cols], w_up.at[:, cols], sems.at[1 + tile]).wait()
        return cols

    def wait_down(tile):
        rows = pl.ds(pl.multiple_of(tile * FF_TILE, FF_TILE), FF_TILE)
        pltpu.make_async_copy(
            down_own.at[0, rows], w_down.at[rows], sems.at[1 + tiles + tile]
        ).wait()
        return rows

    return wait_out, wait_up, wait_down


GELU_SCALE = 0.7978845608028654
GELU_CUBE = 0.044715


def out_part(block, shard_len, count):
    chan = D // count

    def body(sc, x_ref, st_ref, p_ref, bias_ref, *rest):
        ins, rest = rest[:count], rest[count:]
        pairs = (rest[0:2], rest[2:4], rest[4:6])
        result_ref, residual_ref, gated_ref, normed_ref, hidden_ref, slope_ref, cmix_ref = rest[6:13]
        turned, w_out, w_up, w_down, sems = rest[13:]
        wait_out, wait_up, wait_down = fetch_mlp(
            sc[0] == block, pairs, (w_out, w_up, w_down), sems, True
        )
        masks = place_masks(sc, shard_len, shard_len)
        conv = token_major(sc, ins, turned, chan)
        signal = short_conv(st_ref, p_ref, 2, masks) * short_conv(st_ref, p_ref, 1, masks)
        cmix = conv + p_ref[21:22, :] * signal
        cmix_ref[...] = cmix
        gated = (cmix * short_conv(st_ref, p_ref, 0, masks)).astype(bf16)
        gated_ref[...] = gated
        wait_out()
        residual = x_ref[...].astype(f32) + dot(gated, w_out[...]) + p_ref[3:4, :]
        residual_ref[...] = residual
        unit, _ = norm_stats(residual)
        normed_ref[...] = (unit * p_ref[1:2, :] + p_ref[4:5, :]).astype(bf16)
        result_ref[...] = residual + p_ref[5:6, :]

        @pl.loop(0, FF // FF_TILE)
        def _(tile):
            cols = wait_up(tile)
            pre = dot(normed_ref[...], w_up[:, cols]) + bias_ref[:, cols]
            square = pre * pre
            bent = jnp.tanh(GELU_SCALE * pre * (1.0 + GELU_CUBE * square))
            half = 0.5 * (1.0 + bent)
            slope = half + (0.5 * GELU_SCALE) * pre * (1.0 - bent * bent) * (
                1.0 + 3.0 * GELU_CUBE * square
            )
            hidden = (pre * half).astype(bf16)
            hidden_ref[:, cols] = hidden
            slope_ref[:, cols] = slope.astype(bf16)
            rows = wait_down(tile)
            result_ref[...] += dot(hidden, w_down[rows, :])

    def call(sc, x, st, params, up_bias, ins, weights):
        return run(
            body,
            [
                ((shard_len, D), f32),
                ((shard_len, D), f32),
                ((shard_len, D), bf16),
                ((shard_len, D), bf16),
                ((shard_len, FF), bf16),
                ((shard_len, FF), bf16),
                ((shard_len, D), f32),
            ],
            (sc, x, st, params, up_bias, *ins, *weights),
            [SMEM] + [VMEM] * (4 + count) + [ANY] * 6,
            [pltpu.VMEM((D, shard_len), bf16)] + weight_scratch(),
            f"out_part_{block}",
            2 * shard_len * D * (D + 2 * FF),
            D * (D + 2 * FF) * 2,
        )

    return call


def out_back(block, shard_len, count):
    chan = D // count

    def body(sc, grad_ref, residual_ref, slope_ref, st_ref, cmix_ref, p_ref, *rest):
        pairs = (rest[0:2], rest[2:4], rest[4:6])
        d_pre_ref, gm_ref, dres_ref, gb_ref, dg_ref, vec_ref, dub_ref = rest[6:13]
        outs, rest = rest[13 : 13 + count], rest[13 + count :]
        turned, w_out, w_up, w_down, sems, total = rest
        wait_out, wait_up, wait_down = fetch_mlp(
            sc[0] == block, pairs, (w_out, w_up, w_down), sems, False
        )
        grad = grad_ref[...].astype(f32)
        gm = grad.astype(bf16)
        gm_ref[...] = gm
        total[...] = jnp.zeros_like(total)

        @pl.loop(0, FF // FF_TILE)
        def _(tile):
            rows = wait_down(tile)
            d_hidden = dot(gm_ref[...], w_down[rows, :], NT)
            d_pre = (d_hidden * slope_ref[:, rows].astype(f32)).astype(bf16)
            d_pre_ref[:, rows] = d_pre
            dub_ref[:, rows] = jnp.broadcast_to(col_sum(d_pre.astype(f32)), (8, FF_TILE))
            cols = wait_up(tile)
            total[...] += dot(d_pre, w_up[:, cols], NT)

        d_normed = total[...]
        unit, scale = norm_stats(residual_ref[...])
        d_res = grad + norm_back(d_normed, p_ref[1:2, :], unit, scale)
        dres_ref[...] = d_res
        gb = d_res.astype(bf16)
        gb_ref[...] = gb
        wait_out()
        dg = dot(gb, w_out[...], NT).astype(bf16)
        dg_ref[...] = dg
        masks = place_masks(sc, shard_len, shard_len)
        d_conv = dg.astype(f32) * short_conv(st_ref, p_ref, 0, masks)
        turned[...] = d_conv.T.astype(bf16)
        for step in range(count):
            outs[step][...] = turned[rows_at((sc[1] ^ step) * chan, chan), :]
        vec_ref[...] = jnp.concatenate(
            [
                col_sum(d_normed * unit),
                col_sum(d_normed),
                col_sum(gb.astype(f32)),
                col_sum(gm.astype(f32)),
                jnp.zeros((4, D), f32),
            ],
            axis=0,
        )

    def call(sc, grad, residual, slope, st, cmix, params, weights):
        return run(
            body,
            [
                ((shard_len, FF), bf16),
                ((shard_len, D), bf16),
                ((shard_len, D), f32),
                ((shard_len, D), bf16),
                ((shard_len, D), bf16),
                ((8, D), f32),
                ((8, FF), f32),
            ]
            + [((chan, shard_len), bf16)] * count,
            (sc, grad, residual, slope, st, cmix, params, *weights),
            [SMEM] + [VMEM] * 6 + [ANY] * 6,
            [pltpu.VMEM((D, shard_len), bf16)]
            + weight_scratch()
            + [pltpu.VMEM((shard_len, D), f32)],
            f"out_back_{block}",
            2 * shard_len * D * (D + 2 * FF),
            D * (D + 2 * FF) * 2,
        )

    return call


def short_back(block, shard_len, count):
    chan = D // count

    def body(sc, st_ref, dg_ref, cmix_ref, p_ref, *rest):
        ins = rest[:count]
        ds_ref, head_ref, vec_ref, turned = rest[count:]
        masks = place_masks(sc, shard_len, shard_len)
        d_signal = token_major(sc, ins, turned, chan)
        dg = dg_ref[...].astype(f32)
        d_conv = dg * short_conv(st_ref, p_ref, 0, masks)
        inner = short_conv(st_ref, p_ref, 1, masks)
        value = short_conv(st_ref, p_ref, 2, masks)
        d_signal = d_signal + p_ref[21:22, :] * d_conv
        rows = [None] * 16
        rows[12] = col_sum(d_conv * value * inner)
        for stream, d_short in enumerate((dg * cmix_ref[...], d_signal * value, d_signal * inner)):
            cols = slice(stream * D, (stream + 1) * D)
            ds_ref[:, cols] = d_short
            head_ref[:, cols] = d_short[:HALO]
            zero, one, two = shifted(st_ref[:, cols])
            rows[stream] = col_sum(d_short * zero)
            rows[3 + stream] = col_sum(d_short * (one * masks[0]))
            rows[6 + stream] = col_sum(d_short * (two * masks[1]))
            rows[9 + stream] = col_sum(d_short)
        for index in range(13, 16):
            rows[index] = jnp.zeros((1, D), f32)
        vec_ref[...] = jnp.concatenate(rows, axis=0)

    def call(sc, st, dg, cmix, params, ins):
        return run(
            body,
            [((shard_len, 3 * D), f32), ((HALO, 3 * D), f32), ((16, D), f32)],
            (sc, st, dg, cmix, params, *ins),
            [SMEM] + [VMEM] * (4 + count),
            [pltpu.VMEM((D, shard_len), bf16)],
            f"short_back_{block}",
            40 * shard_len * D,
            shard_len * D * 20,
        )

    return call


def in_back(block, shard_len):
    def body(sc, ds_ref, halo_ref, x_ref, dres_ref, p_ref, own, rcv, dst_ref, dx_ref, vec_ref, weight, sems):
        wait = fetch_in(sc[0] == block, own, rcv, weight, sems)
        long = shard_len + HALO
        one, two = place_masks(sc, long, shard_len)
        d_normed = jnp.zeros((shard_len, D), f32)
        rows = []
        for stream in range(3):
            cols = slice(stream * D, (stream + 1) * D)
            ext = jnp.concatenate([ds_ref[:, cols], halo_ref[:, cols]], axis=0)
            d_stream = (
                mix_row(p_ref, 1, stream) * ext[:shard_len]
                + mix_row(p_ref, 2, stream) * pltpu.roll(ext * one, long - 1, 0)[:shard_len]
                + mix_row(p_ref, 3, stream) * pltpu.roll(ext * two, long - 2, 0)[:shard_len]
            ).astype(bf16)
            dst_ref[:, cols] = d_stream
            rows.append(col_sum(d_stream.astype(f32)))
            wait(stream)
            d_normed = d_normed + dot(d_stream, weight[:, cols], NT)
        unit, scale = norm_stats(x_ref[...].astype(f32))
        dx_ref[...] = dres_ref[...] + norm_back(d_normed, p_ref[0:1, :], unit, scale)
        vec_ref[...] = jnp.concatenate(
            [col_sum(d_normed * unit), col_sum(d_normed)] + rows + [jnp.zeros((3, D), f32)], axis=0
        )

    def call(sc, d_short, halo, x, d_res, params, own, rcv):
        return run(
            body,
            [((shard_len, 3 * D), bf16), ((shard_len, D), f32), ((8, D), f32)],
            (sc, d_short, halo, x, d_res, params, own, rcv),
            [SMEM] + [VMEM] * 5 + [ANY] * 2,
            [pltpu.VMEM((D, 3 * D), bf16), pltpu.SemaphoreType.DMA((3,))],
            f"in_back_{block}",
            2 * shard_len * D * 3 * D,
            D * 3 * D * 2,
        )

    return call


def weight_grad(name, rows, cols, shard_len):
    chunk = 384 if rows % 384 == 0 else rows

    def body(g_own, g_rcv, a_own, a_rcv, out_ref):
        @pl.loop(0, rows // chunk)
        def _(step):
            here = pl.ds(pl.multiple_of(step * chunk, chunk), chunk)
            out_ref[here, :] = (
                dot(g_own[:, here], a_own[...], TN) + dot(g_rcv[:, here], a_rcv[...], TN)
            ).astype(bf16)

    def call(*ins):
        return run(
            body,
            [((rows, cols), bf16)],
            ins,
            [VMEM] * 4,
            [],
            name,
            4 * shard_len * rows * cols,
            rows * cols * 2,
        )[0]

    return call


def pairs(count, step):
    return [(index, index ^ step) for index in range(count)]


def swap(value):
    return lax.ppermute(value, "section", pairs(2, 1))


def exchange(chunks):
    count = len(chunks)
    return [chunks[0]] + [
        lax.ppermute(chunks[step], "seq", pairs(count, step)) for step in range(1, count)
    ]


def add_round(first, second):
    return (first.astype(f32) + second.astype(f32)).astype(bf16)


def scatter_sum(value, low_first):
    dp, count = value.shape[0], value.shape[1]
    bits = dp.bit_length() - 1
    index = lax.axis_index("dp")
    value = value.reshape((2,) * bits + value.shape[1:])
    order = list(range(bits))
    if low_first:
        order = order[::-1]
    axes = list(range(bits))
    for bit in order:
        axis = axes.index(bit)
        weight = 1 << (bits - 1 - bit)
        mine = (index // weight) % 2
        send = lax.dynamic_index_in_dim(value, 1 - mine, axis, keepdims=False)
        keep = lax.dynamic_index_in_dim(value, mine, axis, keepdims=False)
        got = lax.ppermute(send, "dp", pairs(dp, weight))
        value = add_round(keep, got)
        axes.remove(bit)
    place = lax.axis_index("seq")
    total = lax.dynamic_index_in_dim(value, place, 0, keepdims=False).astype(f32)
    for step in range(1, count):
        part = lax.dynamic_index_in_dim(value, place ^ step, 0, keepdims=False)
        total = total + lax.ppermute(part, "seq", pairs(count, step)).astype(f32)
    return total


def sum_all(value):
    value = value + swap(value)
    for axis in ("dp", "seq"):
        count = lax.axis_size(axis)
        step = 1
        while step < count:
            value = value + lax.ppermute(value, axis, pairs(count, step))
            step *= 2
    return value


def mat(spec, left, right):
    return jnp.einsum(spec, left, right, precision=highest, preferred_element_type=f32)


def filter_state(net, last, decay, pos, window):
    first_w, inner_b, second_w = net[:EMB], net[EMB : EMB + 2], net[EMB + 2 :]
    pre_a = mat("ef,en->fn", first_w, pos) + inner_b[0][:, None]
    hid_a = jnp.sin(pre_a)
    pre_b = mat("gf,gn->fn", second_w, hid_a) + inner_b[1][:, None]
    hid_b = jnp.sin(pre_b)
    taps = mat("fc,fn->cn", last, hid_b) * decay
    blocks = taps.reshape(taps.shape[0], NB, BLK)
    filt = mat("cmn,nk->mck", blocks, window[BLK:])
    behind = mat("cmn,nk->mck", blocks[:, :-1], window[:BLK])
    filt = filt + jnp.pad(behind, ((1, 0), (0, 0), (0, 0)))
    energy = taps * taps
    share = jnp.sum(jnp.sum(energy[:, LONG_LAG:], axis=1) / (jnp.sum(energy, axis=1) + 1e-06))
    return filt, share, (pre_a, hid_a, pre_b, hid_b, second_w)


def filter_back(d_filt, state, last, decay, pos, window):
    pre_a, hid_a, pre_b, hid_b, second_w = state
    ahead = jnp.pad(d_filt[1:], ((0, 1), (0, 0), (0, 0)))
    d_taps = mat("mck,nk->cmn", d_filt, window[BLK:]) + mat("mck,nk->cmn", ahead, window[:BLK])
    d_out = d_taps.reshape(last.shape[1], SEQ) * (decay / BLK)
    d_last = mat("fn,cn->fc", hid_b, d_out)
    d_b = mat("fc,cn->fn", last, d_out) * jnp.cos(pre_b)
    d_second = mat("gn,fn->gf", hid_a, d_b)
    d_a = mat("gf,fn->gn", second_w, d_b) * jnp.cos(pre_a)
    d_first = mat("en,fn->ef", pos, d_a)
    d_inner = jnp.stack([jnp.sum(d_a, axis=1), jnp.sum(d_b, axis=1)])
    return d_last, jnp.concatenate([d_first, d_inner, d_second], axis=0)


def local(
    layer_input,
    out_cot,
    doc_lengths,
    norm_gains,
    biases,
    in_weight,
    mix_vecs,
    filt_first,
    filt_inner_bias,
    filt_second,
    filt_last,
    filt_skip,
    out_weight,
    up_weight,
    up_bias,
    down_weight,
):
    count = lax.axis_size("seq")
    dp_count = lax.axis_size("dp")
    section = lax.axis_index("section")
    place = lax.axis_index("seq")
    first = section == 0
    shard_len = layer_input.shape[2]
    chan = D // count
    fwd_hi, fwd_lo, inv_hi, inv_lo, window = block_tables()
    tables = tuple(jnp.asarray(t) for t in (fwd_hi, fwd_lo, inv_hi, inv_lo))
    window = jnp.asarray(window)
    pos = jnp.asarray(position_table())

    def own_micro(value):
        return lax.dynamic_index_in_dim(value, section, 0, keepdims=False)[0]

    x_zero = own_micro(layer_input)
    cot = own_micro(out_cot)
    lengths = own_micro(doc_lengths)
    starts = jnp.cumsum(lengths) - lengths
    sc = jnp.concatenate([jnp.stack([section, place]), starts]).astype(jnp.int32)

    def behind(rows):
        return lax.ppermute(rows, "seq", [(index, index + 1) for index in range(count - 1)])

    def ahead(rows):
        return lax.ppermute(rows, "seq", [(index + 1, index) for index in range(count - 1)])

    halo = behind(x_zero[-HALO:])
    small = jnp.concatenate(
        [
            norm_gains[0],
            biases[0],
            mix_vecs[0].reshape(15, D),
            filt_skip[0],
            up_bias[0].reshape(4, D),
            filt_last[0],
        ],
        axis=0,
    )
    net = jnp.concatenate([filt_first[0], filt_inner_bias[0], filt_second[0]], axis=0)
    small_rcv, net_rcv = swap(small), swap(net)
    rcv_in, rcv_out, rcv_up, rcv_down = (
        swap(in_weight),
        swap(out_weight),
        swap(up_weight),
        swap(down_weight),
    )
    mlp_pairs = (out_weight, rcv_out, up_weight, rcv_up, down_weight, rcv_down)
    params, nets = [], []
    for block in range(2):
        mine = section == block
        params.append(jnp.where(mine, small, small_rcv).astype(f32))
        nets.append(jnp.where(mine, net, net_rcv).astype(f32))
    tokens = [p[:24] for p in params]
    up_biases = [p[22:26].reshape(1, FF) for p in params]
    lasts = [lax.dynamic_slice_in_dim(p[26:90], place * chan, chan, 1) for p in params]
    chan_ids = (jnp.arange(chan, dtype=jnp.int32) + place * chan).astype(f32)
    times = jnp.arange(SEQ, dtype=f32) / SEQ
    decay = jnp.exp(-(3.0 + 12.0 * chan_ids / (D - 1))[:, None] * times[None, :])
    filters = [filter_state(nets[b], lasts[b], decay, pos, window) for b in range(2)]

    x = x_zero
    kept = []
    results = []
    for block in range(2):
        normed, st, *chunks = in_part(block, shard_len, count)(
            sc, x, halo, tokens[block], in_weight, rcv_in
        )
        *chunks, blocks = conv_part(block, shard_len, count)(
            sc, filters[block][0], exchange(chunks), tables
        )
        result, residual, gated, normed_two, hidden, slope, cmix = out_part(
            block, shard_len, count
        )(sc, x, st, tokens[block], up_biases[block], exchange(chunks), mlp_pairs)
        kept.append((x, normed, st, blocks, residual, gated, normed_two, hidden, slope, cmix))
        results.append(result)
        x = result
        if block == 0:
            halo = behind(result[-HALO:])

    def half_pair(value):
        half = value.shape[1] // 2
        mine = lax.dynamic_slice_in_dim(value, section * half, half, 1)
        other = lax.dynamic_slice_in_dim(value, (1 - section) * half, half, 1)
        return mine, swap(other)

    def reduced(name, grads, acts, low_first):
        mine, got = half_pair(acts)
        rows, cols = grads.shape[1], mine.shape[1]
        full = weight_grad(name, rows, cols, shard_len)(grads, swap(grads), mine, got)
        blocked = full.reshape(dp_count, count, rows // (dp_count * count), cols)
        return scatter_sum(blocked, low_first)

    grad = cot
    pieces = [None, None]
    packs = [None, None]
    in_grads = [None, None]
    for block in (1, 0):
        x, normed, st, blocks, residual, gated, normed_two, hidden, slope, cmix = kept[block]
        d_pre, gm, d_res, gb, dg, vec_out, d_up_bias, *chunks = out_back(block, shard_len, count)(
            sc, grad, residual, slope, st, cmix, tokens[block], mlp_pairs
        )
        *chunks, d_filt = conv_back(block, shard_len, count)(
            sc, filters[block][0], blocks, exchange(chunks), tables
        )
        d_short, head, vec_short = short_back(block, shard_len, count)(
            sc, st, dg, cmix, tokens[block], exchange(chunks)
        )
        d_st, d_x, vec_in = in_back(block, shard_len)(
            sc, d_short, ahead(head), x, d_res, tokens[block], in_weight, rcv_in
        )
        in_grads[block] = d_x
        grad = d_x
        d_last, d_net = filter_back(d_filt, filters[block][2], lasts[block], decay, pos, window)
        pieces[block] = (
            reduced(f"down_grad_{block}", gm, hidden, True),
            reduced(f"up_grad_{block}", d_pre, normed_two, False),
            reduced(f"out_grad_{block}", gb, gated, True),
            reduced(f"in_grad_{block}", d_st, normed, False),
        )
        last_full = lax.dynamic_update_slice_in_dim(
            jnp.zeros((FILT, D), f32), d_last, place * chan, 1
        )
        extra = filters[0][1] + 4.0 * filters[1][1] if block == 0 else jnp.zeros((), f32)
        extra = extra / (chan * 2 * dp_count)
        flat = jnp.concatenate([d_net.reshape(-1), extra[None]])
        flat = jnp.pad(flat, (0, 9 * D - flat.shape[0])).reshape(9, D)
        packs[block] = sum_all(
            jnp.concatenate(
                [
                    vec_in[0:1],
                    vec_out[0:1],
                    vec_in[1:2],
                    vec_out[2:3],
                    vec_out[1:2],
                    vec_out[3:4],
                    vec_in[2:5],
                    vec_short[0:12],
                    vec_short[12:13],
                    d_up_bias[0:1].reshape(4, D),
                    last_full,
                    flat,
                ],
                axis=0,
            )
        )

    def choose(values):
        return jnp.where(first, values[0], values[1]), jnp.where(first, values[1], values[0])

    def both_micros(values):
        mine, other = choose(values)
        got = swap(other)
        return jnp.stack([jnp.where(first, mine, got), jnp.where(first, got, mine)])[None, :, None]

    def whole_grad(index, turn):
        mine, other = choose([pieces[0][index], pieces[1][index]])
        got = swap(other)
        full = jnp.concatenate(
            [jnp.where(first, mine, got), jnp.where(first, got, mine)], axis=1
        )
        return full.T[None]

    pack, _ = choose(packs)
    shard = lax.axis_index("dp") * count + place
    shards = dp_count * count

    def columns(value):
        width = value.shape[1] // shards
        return lax.dynamic_slice_in_dim(value, shard * width, width, 1)[None]

    flat = pack[90:99].reshape(-1)
    d_net = flat[: 99 * FILT].reshape(99, FILT)
    penalty = packs[0][90:99].reshape(-1)[99 * FILT]
    return (
        both_micros(results),
        both_micros(in_grads),
        columns(pack[0:2]),
        columns(pack[2:6]),
        whole_grad(3, True),
        columns(pack[6:21].reshape(5, 3 * D)),
        d_net[None, :EMB],
        d_net[None, EMB : EMB + 2],
        d_net[None, EMB + 2 :],
        columns(pack[26:90]),
        columns(pack[21:22]),
        whole_grad(2, True),
        whole_grad(1, True),
        columns(pack[22:26].reshape(1, FF)),
        whole_grad(0, True),
        penalty,
    )


def solution(mesh):
    by_section = P("section")
    shard = P("section", None, ("dp", "seq"))
    tokens = P("section", None, "dp", "seq", None)
    return jax.shard_map(
        local,
        mesh=mesh,
        in_specs=(P(None, "dp", "seq", None), P(None, "dp", "seq", None), P(None, "dp", None))
        + (by_section,) * 13,
        out_specs=(tokens, tokens, shard, shard, shard, shard)
        + (by_section,) * 3
        + (shard,) * 6
        + (P(),),
        check_vma=False,
    )
```

time: 3090 us -> 591 us (0.19)
  waiting for transfers between devices: 1260 us -> 166 us
  matrix products: 1020 us -> 35.1 us
  blocking collectives: 283 us -> 0 us
  local copies, waits for them, and re-layouts: 318 us -> 65.5 us
  Pallas kernels: 0 us -> 161 us
  other arithmetic: 140 us -> 27.6 us
  starting transfers between devices: 35.6 us -> 121 us
    unnamed x17 -> x0, waiting for transfers between devices: 1060 us -> none
    dot_general x86 -> x24, matrix products: 1020 us -> 35.1 us  [mat(): jnp.einsum(spec, left, right, precision=highest, preferred_element_type=f32)]
    all_to_all x6 -> x0, blocking collectives: 190 us -> none  [the longest x2 103 us: local(): lax.all_to_all(d_stream_ch.astype(jnp.bfloat16), 'seq', split_axis=1, con...]
    pallas_call x0 -> x22, Pallas kernels: none -> 161 us  [run(): pl.pallas_call(body, out_shape=[jax.ShapeDtypeStruct(shape, dtype) for sh...]
    ppermute x4 -> x106, waiting for transfers between devices: 9.79 us -> 166 us  [the longest x16 69.7 us: scatter_sum(): got = lax.ppermute(send, 'dp', pairs(dp, weight))]
    reduce_scatter x1 -> x0, waiting for transfers between devices: 123 us -> none  [local(): lax.psum_scatter(summed[4], ('dp', 'seq'), scatter_dimension=2, tiled=True)]
    ppermute x4 -> x106, starting transfers between devices: 5.51 us -> 121 us  [the longest x24 39.3 us: scatter_sum(): total = total + lax.ppermute(part, 'seq', pairs(count, step)).astype(f32)]
    psum x2 -> x0, blocking collectives: 92.8 us -> none  [the longest x1 76.6 us: local(): lax.psum((narrow_total[0], narrow_total[1], narrow_total[2]), ('dp', 'seq'))]
  transfers between devices with their start and end apart: 19 -> 106, of which waited for: 14 -> 37; matrix products, arithmetic and copies ran while one was open for 16% -> 20% of each run, Pallas kernels for 0% -> 26%
where the time goes in v1:
time: 591 us; the launch traced here: 580 us
  waiting for transfers between devices  166 us (28%)
  Pallas kernels  161 us (27%)
  starting transfers between devices  121 us (20%)
  local copies, waits for them, and re-layouts  65.5 us (11%)
  matrix products  35.1 us (6%)
  other arithmetic  27.6 us (5%)
    pallas_call x22, Pallas kernels, run(): pl.pallas_call(body, out_shape=[jax.ShapeDtypeStruct(shape, dtype) for sh...  161 us
    ppermute x16, waiting for transfers between devices, scatter_sum(): got = lax.ppermute(send, 'dp', pairs(dp, weight))  69.7 us
    ppermute x24, starting transfers between devices, scatter_sum(): total = total + lax.ppermute(part, 'seq', pairs(count, step)).astype(f32)  39.3 us
    ppermute x24, waiting for transfers between devices, scatter_sum(): total = total + lax.ppermute(part, 'seq', pairs(count, step)).astype(f32)  35.7 us
    ppermute x24, starting transfers between devices, exchange(): lax.ppermute(chunks[step], 'seq', pairs(count, step))  35.3 us
    dot_general x24, matrix products, mat(): jnp.einsum(spec, left, right, precision=highest, preferred_element_type=f32)  35.1 us
    ppermute x24, waiting for transfers between devices, exchange(): lax.ppermute(chunks[step], 'seq', pairs(count, step))  31.9 us
    ppermute x8, waiting for transfers between devices, sum_all(): value = value + lax.ppermute(value, axis, pairs(count, step))  18.8 us
  transfers between devices with their start and end apart: 106, of which 37 were waited for; matrix products, arithmetic and copies ran while one was open for 20% of the time, Pallas kernels for 26%

profile of v1, /device:TPU:0, one launch (start us, length us, event | category | flops | bytes accessed | tf_op | source)
XLA Modules:
  0.0 580.5 jit_solution(18304790907569729481)
XLA Ops:
  2.7 5.5 collective-permute-start
  33.5 2.9 bitcast_add_fusion.filt
  40.1 5.6 in_part_0.1
  58.3 6.9 %conv_part_0.1 = (bf16[192,256]{1,0:T(8,128)(2,1)}, bf16[192,256]{1,0:T(8,128)(2,1)}, bf16[192,256]{1,0:T(8,128)(2,1)}, bf16[192,256]{1,0:T(8,128)(2,1)}, bf16[8,192,128]{2,1,0:T(8,128)(2,1)}) custom-call(s32[5]{0:T(128)} %pad_add_fusion.sc, f32[8,192,256]{2,1,0:T(8,128)} %bitcast_add_fusion.1.filt, bf16[192,256]{1,0:T(8,128)(2,1)} %get-tuple-element.97.rest_0_, ...), custom_call_target="tpu_custom_call" | custom-call | flops 629145600 | bytes 1572864 | tf_op jit(solution)/shard_map/conv_part_0/pallas_call | solution.py:168
  70.9 6.7 %collective-permute-done.8.rest_2_ = bf16[192,256]{1,0:T(8,128)(2,1)S(1)} collective-permute-done((bf16[192,256]{1,0:T(8,128)(2,1)}, bf16[192,256]{1,0:T(8,128)(2,1)S(1)}, u32[]{:S(2)}, u32[]{:S(2)}) %collective-permute-start.8) | collective-permute-done | bytes 98336 | tf_op jit(solution)/shard_map/ppermute | solution.py:747
  78.3 12.2 %out_part_0.1 = (f32[256,768]{1,0:T(8,128)}, f32[256,768]{1,0:T(8,128)}, bf16[256,768]{1,0:T(8,128)(2,1)}, bf16[256,768]{1,0:T(8,128)(2,1)}, bf16[256,3072]{1,0:...) custom-call(s32[5]{0:T(128)} %pad_add_fusion.sc, bf16[256,768]{1,0:T(8,128)(2,1)} %dynamic-slice_bitcast_fusion.13.x_ref, ...), custom_call_target="tpu_custom_call" | custom-call | flops 2717908992 | bytes 10616832 | tf_op jit(solution)/shard_map/out_part_0/pallas_call | solution.py:168
  91.3 3.7 collective-permute-start.13
  100.1 5.7 in_part_1.1
  107.1 3.2 collective-permute-start.16
  111.8 6.0 %collective-permute-done.15.rest_2_ = bf16[192,256]{1,0:T(8,128)(2,1)S(1)} collective-permute-done((bf16[192,256]{1,0:T(8,128)(2,1)}, bf16[192,256]{1,0:T(8,128)(2,1)S(1)}, u32[]{:S(2)}, u32[]{:S(2)}) %collective-permute-start.15) | collective-permute-done | bytes 98336 | tf_op jit(solution)/shard_map/ppermute | solution.py:747
  118.5 7.1 %conv_part_1.1 = (bf16[192,256]{1,0:T(8,128)(2,1)}, bf16[192,256]{1,0:T(8,128)(2,1)}, bf16[192,256]{1,0:T(8,128)(2,1)}, bf16[192,256]{1,0:T(8,128)(2,1)}, bf16[8,192,128]{2,1,0:T(8,128)(2,1)}) custom-call(s32[5]{0:T(128)} %pad_add_fusion.sc, f32[8,192,256]{2,1,0:T(8,128)} %bitcast_add_fusion.filt, bf16[192,256]{1,0:T(8,128)(2,1)} %get-tuple-element.107.rest_0_, ...), custom_call_target="tpu_custom_call" | custom-call | flops 629145600 | bytes 1572864 | tf_op jit(solution)/shard_map/conv_part_1/pallas_call | solution.py:168
  131.4 6.6 %collective-permute-done.18.rest_2_ = bf16[192,256]{1,0:T(8,128)(2,1)S(1)} collective-permute-done((bf16[192,256]{1,0:T(8,128)(2,1)}, bf16[192,256]{1,0:T(8,128)(2,1)S(1)}, u32[]{:S(2)}, u32[]{:S(2)}) %collective-permute-start.18) | collective-permute-done | bytes 98336 | tf_op jit(solution)/shard_map/ppermute | solution.py:747
  138.6 12.4 %out_part_1.1 = (f32[256,768]{1,0:T(8,128)}, f32[256,768]{1,0:T(8,128)}, bf16[256,768]{1,0:T(8,128)(2,1)}, bf16[256,768]{1,0:T(8,128)(2,1)}, bf16[256,3072]{1,0:...) custom-call(s32[5]{0:T(128)} %pad_add_fusion.sc, f32[256,768]{1,0:T(8,128)} %get-tuple-element.105.x_ref, ...), custom_call_target="tpu_custom_call" | custom-call | flops 2717908992 | bytes 10616832 | tf_op jit(solution)/shard_map/out_part_1/pallas_call | solution.py:168
  154.1 12.0 %out_back_1.1 = (bf16[256,3072]{1,0:T(8,128)(2,1)}, bf16[256,768]{1,0:T(8,128)(2,1)}, f32[256,768]{1,0:T(8,128)}, bf16[256,768]{1,0:T(8,128)(2,1)}, bf16[256,768...) custom-call(s32[5]{0:T(128)} %pad_add_fusion.sc, ...), custom_call_target="tpu_custom_call" | custom-call | flops 2717908992 | bytes 10616832 | tf_op jit(solution)/shard_map/out_back_1/pallas_call | solution.py:168
  175.0 5.0 collective-permute-done.22.rest_2_
  180.7 9.7 %conv_back_1.1 = (bf16[192,256]{1,0:T(8,128)(2,1)}, bf16[192,256]{1,0:T(8,128)(2,1)}, bf16[192,256]{1,0:T(8,128)(2,1)}, bf16[192,256]{1,0:T(8,128)(2,1)}, f32[8,192,256]{2,1,0:T(8,128)}) custom-call(s32[5]{0:T(128)} %pad_add_fusion.sc, f32[8,192,256]{2,1,0:T(8,128)} %bitcast_add_fusion.filt, bf16[8,192,128]{2,1,0:T(8,128)(2,1)} %get-tuple-element.120.blocks, ...), custom_call_target="tpu_custom_call" | custom-call | flops 880803840 | bytes 3145728 | tf_op jit(solution)/shard_map/conv_back_1/pallas_call | solution.py:168
  204.5 7.5 %short_back_1.1 = (f32[256,2304]{1,0:T(8,128)}, f32[16,2304]{1,0:T(8,128)}, f32[16,768]{1,0:T(8,128)}) custom-call(s32[5]{0:T(128)} %pad_add_fusion.sc, bf16[272,2304]{1,0:T(8,128)(2,1)} %get-tuple-element.106.st_ref, bf16[256,768]{1,0:T(8,128)(2,1)} %get-tuple-element.119.dg_ref, f32[256,768]{1,0:T(8,128)} %get-tuple-element.118.cmix_ref, ...), custom_call_target="tpu_custom_call" | custom-call | flops 7864320 | bytes 3932160 | tf_op jit(solution)/shard_map/short_back_1/pallas_call | solution.py:168
  215.0 4.8 collective-permute-done.27.halo_ref
  220.5 6.9 %in_back_1.1 = (bf16[256,2304]{1,0:T(8,128)(2,1)}, f32[256,768]{1,0:T(8,128)}, f32[8,768]{1,0:T(8,128)}) custom-call(s32[5]{0:T(128)} %pad_add_fusion.sc, f32[256,2304]{1,0:T(8,128)} %get-tuple-element.129.ds_ref, f32[16,2304]{1,0:T(8,128)} %copy-done.71, f32[256,768]{1,0:T(8,128)} %get-tuple-element.105.x_ref, f32[256,768]{1,0:T(8,128)} %get-tuple-element.131.dres_ref, ...), custom_call_target="tpu_custom_call" | custom-call | flops 905969664 | bytes 3538944 | tf_op jit(solution)/shard_map/in_back_1/pallas_call | solution.py:168
  228.1 12.0 %out_back_0.1 = (bf16[256,3072]{1,0:T(8,128)(2,1)}, bf16[256,768]{1,0:T(8,128)(2,1)}, f32[256,768]{1,0:T(8,128)}, bf16[256,768]{1,0:T(8,128)(2,1)}, bf16[256,768...) custom-call(s32[5]{0:T(128)} %pad_add_fusion.sc, ...), custom_call_target="tpu_custom_call" | custom-call | flops 2717908992 | bytes 10616832 | tf_op jit(solution)/shard_map/out_back_0/pallas_call | solution.py:168
  245.2 3.3 collective-permute-start.30
  253.8 9.6 %conv_back_0.1 = (bf16[192,256]{1,0:T(8,128)(2,1)}, bf16[192,256]{1,0:T(8,128)(2,1)}, bf16[192,256]{1,0:T(8,128)(2,1)}, bf16[192,256]{1,0:T(8,128)(2,1)}, f32[8,192,256]{2,1,0:T(8,128)}) custom-call(s32[5]{0:T(128)} %pad_add_fusion.sc, f32[8,192,256]{2,1,0:T(8,128)} %bitcast_add_fusion.1.filt, bf16[8,192,128]{2,1,0:T(8,128)(2,1)} %get-tuple-element.137.blocks, ...), custom_call_target="tpu_custom_call" | custom-call | flops 880803840 | bytes 3145728 | tf_op jit(solution)/shard_map/conv_back_0/pallas_call | solution.py:168
  277.2 7.3 %short_back_0.1 = (f32[256,2304]{1,0:T(8,128)}, f32[16,2304]{1,0:T(8,128)}, f32[16,768]{1,0:T(8,128)}) custom-call(s32[5]{0:T(128)} %pad_add_fusion.sc, bf16[272,2304]{1,0:T(8,128)(2,1)} %get-tuple-element.96.st_ref, bf16[256,768]{1,0:T(8,128)(2,1)} %get-tuple-element.136.dg_ref, f32[256,768]{1,0:T(8,128)} %get-tuple-element.135.cmix_ref, ...), custom_call_target="tpu_custom_call" | custom-call | flops 7864320 | bytes 3932160 | tf_op jit(solution)/shard_map/short_back_0/pallas_call | solution.py:168
  289.3 3.1 collective-permute-done.34.halo_ref
  293.9 6.9 %in_back_0.1 = (bf16[256,2304]{1,0:T(8,128)(2,1)}, f32[256,768]{1,0:T(8,128)}, f32[8,768]{1,0:T(8,128)}) custom-call(s32[5]{0:T(128)} %pad_add_fusion.sc, f32[256,2304]{1,0:T(8,128)} %get-tuple-element.146.ds_ref, f32[16,2304]{1,0:T(8,128)} %copy-done.70, bf16[256,768]{1,0:T(8,128)(2,1)} %dynamic-slice_bitcast_fusion.13.x_ref, ...), custom_call_target="tpu_custom_call" | custom-call | flops 905969664 | bytes 3538944 | tf_op jit(solution)/shard_map/in_back_0/pallas_call | solution.py:168
  308.5 4.7 down_grad_0.1
  319.2 6.4 %collective-permute-done.63 = bf16[2,4,48,384]{3,2,1,0:T(8,128)(2,1)S(1)} collective-permute-done((bf16[2,4,48,384]{3,2,1,0:T(8,128)(2,1)S(1)}, bf16[2,4,48,384]{3,2,1,0:T(8,128)(2,1)S(1)}, u32[]{:S(2)}, u32[]{:S(2)}) %collective-permute-start.63) | collective-permute-done | bytes 294944 | tf_op jit(solution)/shard_map/ppermute | solution.py:770
  327.3 3.5 collective-permute-done.71
  346.4 4.8 down_grad_1.1
  358.2 4.2 collective-permute-done.37
  367.5 6.5 %collective-permute-done.44 = f32[99,768]{1,0:T(8,128)S(1)} collective-permute-done((f32[99,768]{1,0:T(8,128)S(1)}, f32[99,768]{1,0:T(8,128)S(1)}, u32[]{:S(2)}, u32[]{:S(2)}) %collective-permute-start.44) | collective-permute-done | bytes 304160 | tf_op jit(solution)/shard_map/ppermute | solution.py:787
  375.6 5.3 in_grad_1.1
  383.3 6.7 %up_grad_1.1 = bf16[3072,384]{1,0:T(8,128)(2,1)} custom-call(bf16[256,3072]{1,0:T(8,128)(2,1)} %get-tuple-element.170.g_own, bf16[256,3072]{1,0:T(8,128)(2,1)} %collective-permute-done.83.g_rcv, bf16[256,384]{1,0:T(8,128)(2,1)} %get-tuple-element.267.a_own, bf16[256,384]{1,0:T(8,128)(2,1)} %copy-done.58), custom_call_target="tpu_custom_call" | custom-call | flops 1207959552 | bytes 2359296 | tf_op jit(solution)/shard_map/up_grad_1/pallas_call | solution.py:168
  395.5 5.4 in_grad_0.1
  406.0 6.9 %up_grad_0.1 = bf16[3072,384]{1,0:T(8,128)(2,1)} custom-call(bf16[256,3072]{1,0:T(8,128)(2,1)} %get-tuple-element.168.g_own, bf16[256,3072]{1,0:T(8,128)(2,1)} %copy-done.35, bf16[256,384]{1,0:T(8,128)(2,1)} %get-tuple-element.269.a_own, bf16[256,384]{1,0:T(8,128)(2,1)} %copy-done.59), custom_call_target="tpu_custom_call" | custom-call | flops 1207959552 | bytes 2359296 | tf_op jit(solution)/shard_map/up_grad_0/pallas_call | solution.py:168
  428.8 5.2 collective-permute-done.40
  441.0 22.8 %collective-permute-done.94 = bf16[4,48,1536]{2,1,0:T(8,128)(2,1)} collective-permute-done((bf16[4,48,1536]{2,1,0:T(8,128)(2,1)}, bf16[4,48,1536]{2,1,0:T(8,128)(2,1)}, u32[]{:S(2)}, u32[]{:S(2)}) %collective-permute-start.94) | collective-permute-done | bytes 589856 | tf_op jit(solution)/shard_map/ppermute | solution.py:770
  467.4 8.1 %collective-permute-done.101 = bf16[4,48,1536]{2,1,0:T(8,128)(2,1)} collective-permute-done((bf16[4,48,1536]{2,1,0:T(8,128)(2,1)}, bf16[4,48,1536]{2,1,0:T(8,128)(2,1)}, u32[]{:S(2)}, u32[]{:S(2)}) %collective-permute-start.101) | collective-permute-done | bytes 589856 | tf_op jit(solution)/shard_map/ppermute | solution.py:770
  481.7 4.3 collective-permute-done.96
  491.0 5.8 collective-permute-done.103
  497.1 3.1 collective-permute-done.48
  504.5 3.4 collective-permute-start.57
  510.7 12.5 %collective-permute-done.78 = bf16[2,4,192,384]{3,2,1,0:T(8,128)(2,1)S(1)} collective-permute-done((bf16[2,4,192,384]{3,2,1,0:T(8,128)(2,1)S(1)}, bf16[2,4,192,384]{3,2,1,0:T(8,128)(2,1)S(1)}, u32[]{:S(2)}, u32[]{:S(2)}) %collective-permute-start.78) | collective-permute-done | bytes 1179680 | tf_op jit(solution)/shard_map/ppermute | solution.py:770
  530.0 8.9 %collective-permute-done.79 = bf16[4,192,384]{2,1,0:T(8,128)(2,1)S(1)} collective-permute-done((bf16[4,192,384]{2,1,0:T(8,128)(2,1)S(1)}, bf16[4,192,384]{2,1,0:T(8,128)(2,1)S(1)}, u32[]{:S(2)}, u32[]{:S(2)}) %collective-permute-start.79) | collective-permute-done | bytes 589856 | tf_op jit(solution)/shard_map/ppermute | solution.py:770
  549.7 6.5 %collective-permute-start.80 = (bf16[192,384]{1,0:T(8,128)(2,1)S(1)}, bf16[192,384]{1,0:T(8,128)(2,1)S(1)}, u32[]{:S(2)}, u32[]{:S(2)}) collective-permute-start(bf16[192,384]{1,0:T(8,128)(2,1)S(1)} %get-tuple-element.257), channel_id=1, source_target_pairs={{0,1},{1,0},{2,3},{3,2},{4,5},{5,4},{6,7},{7,6},{8,9},{9,8},{10,11... | collective-permute-start | bytes 442376 | tf_op jit(solution)/shard_map/ppermute | solution.py:777
  556.3 3.1 collective-permute-done.51
  561.5 10.6 %collective-permute-done.88 = bf16[192,384]{1,0:T(8,128)(2,1)S(1)} collective-permute-done((bf16[192,384]{1,0:T(8,128)(2,1)S(1)}, bf16[192,384]{1,0:T(8,128)(2,1)S(1)}, u32[]{:S(2)}, u32[]{:S(2)}) %collective-permute-start.88) | collective-permute-done | bytes 147488 | tf_op jit(solution)/shard_map/ppermute | solution.py:777
  572.1 5.3 collective-permute-done.81
  (584 shorter events, 249.6 us)
Async XLA Ops:
  2.7 37.4 %collective-permute-start = (bf16[16,768]{1,0:T(8,128)(2,1)}, bf16[16,768]{1,0:T(8,128)(2,1)}, u32[]{:S(2)}, u32[]{:S(2)}) collective-permute-start(bf16[16,768]{1,0:T(8,128)(2,1)} %dynamic-slice_bitcast_fusion.42), channel_id=1, source_target_pairs={{0,1},{1,2},{2,3},{4,5},{5,6},{6,7},{8,9},{9,10},{10,11},{12,13},{... | collective-permute-start | bytes 73736 | tf_op jit(solution)/shard_map/ppermute | solution.py:866
  13.8 63.8 %collective-permute-start.11 = (bf16[1,768,3072]{2,1,0:T(8,128)(2,1)}, bf16[1,768,3072]{2,1,0:T(8,128)(2,1)}, u32[]{:S(2)}, u32[]{:S(2)}) collective-permute-start(bf16[1,768,3072]{2,1,0:T(8,128)(2,1)} %rest_2_.3), channel_id=1, source_target_pairs={{0,16},{16,0},{1,17},{17,1},{2,18},{18,2},{3,19},{19,3},{4,20},{20... | collective-permute-start | bytes 14155784 | tf_op jit(solution)/shard_map/ppermute | solution.py:741
  13.9 63.7 %collective-permute-start.12 = (bf16[1,3072,768]{2,1,0:T(8,128)(2,1)}, bf16[1,3072,768]{2,1,0:T(8,128)(2,1)}, u32[]{:S(2)}, u32[]{:S(2)}) collective-permute-start(bf16[1,3072,768]{2,1,0:T(8,128)(2,1)} %rest_4_.11), channel_id=1, source_target_pairs={{0,16},{16,0},{1,17},{17,1},{2,18},{18,2},{3,19},{19,3},{4,20},{20... | collective-permute-start | bytes 14155784 | tf_op jit(solution)/shard_map/ppermute | solution.py:741
  16.7 23.4 %collective-permute-start.2 = (bf16[1,768,2304]{2,1,0:T(8,128)(2,1)}, bf16[1,768,2304]{2,1,0:T(8,128)(2,1)}, u32[]{:S(2)}, u32[]{:S(2)}) collective-permute-start(bf16[1,768,2304]{2,1,0:T(8,128)(2,1)} %own.7), channel_id=1, source_target_pairs={{0,16},{16,0},{1,17},{17,1},{2,18},{18,2},{3,19},{19,3},{4,20},{20... | collective-permute-start | bytes 10616840 | tf_op jit(solution)/shard_map/ppermute | solution.py:741
  24.1 44.1 %collective-permute-start.10 = (bf16[1,768,768]{2,1,0:T(8,128)(2,1)S(1)}, bf16[1,768,768]{2,1,0:T(8,128)(2,1)S(1)}, u32[]{:S(2)}, u32[]{:S(2)}) collective-permute-start(bf16[1,768,768]{2,1,0:T(8,128)(2,1)S(1)} %copy-done.4), channel_id=1, source_target_pairs={{0,16},{16,0},{1,17},{17,1},{2,18},{18,2},{3,19},{19,3},{4,20},{20... | collective-permute-start | bytes 3538952 | tf_op jit(solution)/shard_map/ppermute | solution.py:741
  96.8 207.2 %collective-permute-start.62 = (bf16[256,384]{1,0:T(8,128)(2,1)}, bf16[256,384]{1,0:T(8,128)(2,1)}, u32[]{:S(2)}, u32[]{:S(2)}) collective-permute-start(bf16[256,384]{1,0:T(8,128)(2,1)} %get-tuple-element.272), channel_id=1, source_target_pairs={{0,16},{16,0},{1,17},{17,1},{2,18},{18,2},{3,19},{19,3},{4,20},{20... | collective-permute-start | bytes 589832 | tf_op jit(solution)/shard_map/ppermute | solution.py:741
  152.9 92.4 %collective-permute-start.69 = (bf16[256,384]{1,0:T(8,128)(2,1)}, bf16[256,384]{1,0:T(8,128)(2,1)}, u32[]{:S(2)}, u32[]{:S(2)}) collective-permute-start(bf16[256,384]{1,0:T(8,128)(2,1)} %get-tuple-element.270), channel_id=1, source_target_pairs={{0,16},{16,0},{1,17},{17,1},{2,18},{18,2},{3,19},{19,3},{4,20},{20... | collective-permute-start | bytes 589832 | tf_op jit(solution)/shard_map/ppermute | solution.py:741
  190.4 13.5 %collective-permute-start.24 = (bf16[192,256]{1,0:T(8,128)(2,1)}, bf16[192,256]{1,0:T(8,128)(2,1)S(1)}, u32[]{:S(2)}, u32[]{:S(2)}) collective-permute-start(bf16[192,256]{1,0:T(8,128)(2,1)} %get-tuple-element.126), channel_id=1, source_target_pairs={{0,1},{1,0},{2,3},{3,2},{4,5},{5,4},{6,7},{7,6},{8,9},{9,8},{10,11... | collective-permute-start | bytes 294920 | tf_op jit(solution)/shard_map/ppermute | solution.py:747
  203.9 44.7 %collective-permute-start.68 = (bf16[256,768]{1,0:T(8,128)(2,1)S(1)}, bf16[256,768]{1,0:T(8,128)(2,1)}, u32[]{:S(2)}, u32[]{:S(2)}) collective-permute-start(bf16[256,768]{1,0:T(8,128)(2,1)S(1)} %copy-done.47), channel_id=1, source_target_pairs={{0,16},{16,0},{1,17},{17,1},{2,18},{18,2},{3,19},{19,3},{4,20},{20... | collective-permute-start | bytes 1179656 | tf_op jit(solution)/shard_map/ppermute | solution.py:741
  248.6 38.9 %collective-permute-start.41 = (f32[99,768]{1,0:T(8,128)S(1)}, f32[99,768]{1,0:T(8,128)S(1)}, u32[]{:S(2)}, u32[]{:S(2)}) collective-permute-start(f32[99,768]{1,0:T(8,128)S(1)} %concatenate.49), channel_id=1, source_target_pairs={{0,16},{16,0},{1,17},{17,1},{2,18},{18,2},{3,19},{19,3},{4,20},{20... | collective-permute-start | bytes 912392 | tf_op jit(solution)/shard_map/ppermute | solution.py:741
  276.7 30.8 %collective-permute-start.92 = (bf16[256,1536]{1,0:T(8,128)(2,1)}, bf16[256,1536]{1,0:T(8,128)(2,1)}, u32[]{:S(2)}, u32[]{:S(2)}) collective-permute-start(bf16[256,1536]{1,0:T(8,128)(2,1)} %get-tuple-element.236), channel_id=1, source_target_pairs={{0,16},{16,0},{1,17},{17,1},{2,18},{18,2},{3,19},{19,3},{4,20},{20... | collective-permute-start | bytes 2359304 | tf_op jit(solution)/shard_map/ppermute | solution.py:741
  276.7 27.7 %collective-permute-start.61 = (bf16[256,768]{1,0:T(8,128)(2,1)}, bf16[256,768]{1,0:T(8,128)(2,1)}, u32[]{:S(2)}, u32[]{:S(2)}) collective-permute-start(bf16[256,768]{1,0:T(8,128)(2,1)} %get-tuple-element.164.g_own), channel_id=1, source_target_pairs={{0,16},{16,0},{1,17},{17,1},{2,18},{18,2},{3,19},{19,3},{4,20},{20... | collective-permute-start | bytes 1179656 | tf_op jit(solution)/shard_map/ppermute | solution.py:741
  288.2 19.5 %collective-permute-start.91 = (bf16[256,768]{1,0:T(8,128)(2,1)S(1)}, bf16[256,768]{1,0:T(8,128)(2,1)}, u32[]{:S(2)}, u32[]{:S(2)}) collective-permute-start(bf16[256,768]{1,0:T(8,128)(2,1)S(1)} %copy-done.46), channel_id=1, source_target_pairs={{0,16},{16,0},{1,17},{17,1},{2,18},{18,2},{3,19},{19,3},{4,20},{20... | collective-permute-start | bytes 1179656 | tf_op jit(solution)/shard_map/ppermute | solution.py:741
  304.0 32.0 %collective-permute-start.54 = (bf16[256,384]{1,0:T(8,128)(2,1)}, bf16[256,384]{1,0:T(8,128)(2,1)}, u32[]{:S(2)}, u32[]{:S(2)}) collective-permute-start(bf16[256,384]{1,0:T(8,128)(2,1)} %get-tuple-element.274), channel_id=1, source_target_pairs={{0,16},{16,0},{1,17},{17,1},{2,18},{18,2},{3,19},{19,3},{4,20},{20... | collective-permute-start | bytes 589832 | tf_op jit(solution)/shard_map/ppermute | solution.py:741
  304.4 32.6 %collective-permute-start.98 = (bf16[256,768]{1,0:T(8,128)(2,1)}, bf16[256,768]{1,0:T(8,128)(2,1)S(1)}, u32[]{:S(2)}, u32[]{:S(2)}) collective-permute-start(bf16[256,768]{1,0:T(8,128)(2,1)} %get-tuple-element.174.g_own), channel_id=1, source_target_pairs={{0,16},{16,0},{1,17},{17,1},{2,18},{18,2},{3,19},{19,3},{4,20},{20... | collective-permute-start | bytes 1179656 | tf_op jit(solution)/shard_map/ppermute | solution.py:741
  307.4 30.6 %collective-permute-start.99 = (bf16[256,1536]{1,0:T(8,128)(2,1)S(1)}, bf16[256,1536]{1,0:T(8,128)(2,1)S(1)}, u32[]{:S(2)}, u32[]{:S(2)}) collective-permute-start(bf16[256,1536]{1,0:T(8,128)(2,1)S(1)} %copy-done.44), channel_id=1, source_target_pairs={{0,16},{16,0},{1,17},{17,1},{2,18},{18,2},{3,19},{19,3},{4,20},{20... | collective-permute-start | bytes 2359304 | tf_op jit(solution)/shard_map/ppermute | solution.py:741
  307.8 24.6 %collective-permute-start.42 = (f32[99,768]{1,0:T(8,128)S(1)}, f32[99,768]{1,0:T(8,128)S(1)}, u32[]{:S(2)}, u32[]{:S(2)}) collective-permute-start(f32[99,768]{1,0:T(8,128)S(1)} %add.450), channel_id=1, source_target_pairs={{0,4},{4,0},{8,12},{12,8},{1,5},{5,1},{9,13},{13,9},{2,6},{6,2},{1... | collective-permute-start | bytes 912392 | tf_op jit(solution)/shard_map/ppermute | solution.py:787
  333.1 31.2 %collective-permute-start.53 = (bf16[256,2304]{1,0:T(8,128)(2,1)}, bf16[256,2304]{1,0:T(8,128)(2,1)}, u32[]{:S(2)}, u32[]{:S(2)}) collective-permute-start(bf16[256,2304]{1,0:T(8,128)(2,1)} %get-tuple-element.162.g_own), channel_id=1, source_target_pairs={{0,16},{16,0},{1,17},{17,1},{2,18},{18,2},{3,19},{19,3},{4,20},{20... | collective-permute-start | bytes 3538952 | tf_op jit(solution)/shard_map/ppermute | solution.py:741
  340.0 13.9 %collective-permute-start.43 = (f32[99,768]{1,0:T(8,128)S(1)}, f32[99,768]{1,0:T(8,128)S(1)}, u32[]{:S(2)}, u32[]{:S(2)}) collective-permute-start(f32[99,768]{1,0:T(8,128)S(1)} %add.451), channel_id=1, source_target_pairs={{0,8},{4,12},{8,0},{12,4},{1,9},{5,13},{9,1},{13,5},{2,10},{6,14},... | collective-permute-start | bytes 912392 | tf_op jit(solution)/shard_map/ppermute | solution.py:787
  351.3 31.8 %collective-permute-start.83 = (bf16[256,3072]{1,0:T(8,128)(2,1)S(1)}, bf16[256,3072]{1,0:T(8,128)(2,1)}, u32[]{:S(2)}, u32[]{:S(2)}) collective-permute-start(bf16[256,3072]{1,0:T(8,128)(2,1)S(1)} %copy-done.33), channel_id=1, source_target_pairs={{0,16},{16,0},{1,17},{17,1},{2,18},{18,2},{3,19},{19,3},{4,20},{20... | collective-permute-start | bytes 4718600 | tf_op jit(solution)/shard_map/ppermute | solution.py:741
  356.4 48.1 %collective-permute-start.76 = (bf16[256,3072]{1,0:T(8,128)(2,1)S(1)}, bf16[256,3072]{1,0:T(8,128)(2,1)S(1)}, u32[]{:S(2)}, u32[]{:S(2)}) collective-permute-start(bf16[256,3072]{1,0:T(8,128)(2,1)S(1)} %copy-done.34), channel_id=1, source_target_pairs={{0,16},{16,0},{1,17},{17,1},{2,18},{18,2},{3,19},{19,3},{4,20},{20... | collective-permute-start | bytes 4718600 | tf_op jit(solution)/shard_map/ppermute | solution.py:741
  362.3 32.2 %collective-permute-start.46 = (bf16[256,2304]{1,0:T(8,128)(2,1)}, bf16[256,2304]{1,0:T(8,128)(2,1)}, u32[]{:S(2)}, u32[]{:S(2)}) collective-permute-start(bf16[256,2304]{1,0:T(8,128)(2,1)} %get-tuple-element.160.g_own), channel_id=1, source_target_pairs={{0,16},{16,0},{1,17},{17,1},{2,18},{18,2},{3,19},{19,3},{4,20},{20... | collective-permute-start | bytes 3538952 | tf_op jit(solution)/shard_map/ppermute | solution.py:741
  363.1 52.4 %collective-permute-start.93 = (bf16[2,4,48,1536]{3,2,1,0:T(8,128)(2,1)}, bf16[2,4,48,1536]{3,2,1,0:T(8,128)(2,1)}, u32[]{:S(2)}, u32[]{:S(2)}) collective-permute-start(bf16[2,4,48,1536]{3,2,1,0:T(8,128)(2,1)} %dynamic-slice_bitcast_fusion.1), channel_id=1, source_target_pairs={{0,4},{4,0},{8,12},{12,8},{1,5},{5,1},{9,13},{13,9},{2,6},{6,2},{1... | collective-permute-start | bytes 3538952 | tf_op jit(solution)/shard_map/ppermute | solution.py:770
  374.1 15.9 %collective-permute-start.38 = (f32[99,768]{1,0:T(8,128)S(1)}, f32[99,768]{1,0:T(8,128)S(1)}, u32[]{:S(2)}, u32[]{:S(2)}) collective-permute-start(f32[99,768]{1,0:T(8,128)S(1)} %add.444), channel_id=1, source_target_pairs={{0,8},{4,12},{8,0},{12,4},{1,9},{5,13},{9,1},{13,5},{2,10},{6,14},... | collective-permute-start | bytes 912392 | tf_op jit(solution)/shard_map/ppermute | solution.py:787
  394.6 28.2 %collective-permute-start.100 = (bf16[2,4,48,1536]{3,2,1,0:T(8,128)(2,1)S(1)}, bf16[2,4,48,1536]{3,2,1,0:T(8,128)(2,1)S(1)}, u32[]{:S(2)}, u32[]{:S(2)}) collective-permute-start(bf16[2,4,48,1536]{3,2,1,0:T(8,128)(2,1)S(1)} %copy-done.37), channel_id=1, source_target_pairs={{0,4},{4,0},{8,12},{12,8},{1,5},{5,1},{9,13},{13,9},{2,6},{6,2},{1... | collective-permute-start | bytes 3538952 | tf_op jit(solution)/shard_map/ppermute | solution.py:770
  403.1 74.4 %collective-permute-start.55 = (bf16[2,4,144,384]{3,2,1,0:T(8,128)(2,1)}, bf16[2,4,144,384]{3,2,1,0:T(8,128)(2,1)}, u32[]{:S(2)}, u32[]{:S(2)}) collective-permute-start(bf16[2,4,144,384]{3,2,1,0:T(8,128)(2,1)} %dynamic-slice_bitcast_fusion.4), channel_id=1, source_target_pairs={{0,8},{4,12},{8,0},{12,4},{1,9},{5,13},{9,1},{13,5},{2,10},{6,14},... | collective-permute-start | bytes 2654216 | tf_op jit(solution)/shard_map/ppermute | solution.py:770
  403.6 23.7 %collective-permute-start.45 = (f32[99,768]{1,0:T(8,128)S(1)}, f32[99,768]{1,0:T(8,128)S(1)}, u32[]{:S(2)}, u32[]{:S(2)}) collective-permute-start(f32[99,768]{1,0:T(8,128)S(1)} %add.453), channel_id=1, source_target_pairs={{0,2},{1,3},{2,0},{3,1},{4,6},{5,7},{6,4},{7,5},{8,10},{9,11},{10,... | collective-permute-start | bytes 912392 | tf_op jit(solution)/shard_map/ppermute | solution.py:787
  404.5 97.1 %collective-permute-start.85 = (bf16[2,4,192,384]{3,2,1,0:T(8,128)(2,1)}, bf16[2,4,192,384]{3,2,1,0:T(8,128)(2,1)}, u32[]{:S(2)}, u32[]{:S(2)}) collective-permute-start(bf16[2,4,192,384]{3,2,1,0:T(8,128)(2,1)} %dynamic-slice_bitcast_fusion.2), channel_id=1, source_target_pairs={{0,8},{4,12},{8,0},{12,4},{1,9},{5,13},{9,1},{13,5},{2,10},{6,14},... | collective-permute-start | bytes 3538952 | tf_op jit(solution)/shard_map/ppermute | solution.py:770
  415.5 18.5 %collective-permute-start.40 = (f32[99,768]{1,0:T(8,128)S(1)}, f32[99,768]{1,0:T(8,128)S(1)}, u32[]{:S(2)}, u32[]{:S(2)}) collective-permute-start(f32[99,768]{1,0:T(8,128)S(1)} %add.446), channel_id=1, source_target_pairs={{0,2},{1,3},{2,0},{3,1},{4,6},{5,7},{6,4},{7,5},{8,10},{9,11},{10,... | collective-permute-start | bytes 912392 | tf_op jit(solution)/shard_map/ppermute | solution.py:787
  422.8 41.0 %collective-permute-start.94 = (bf16[4,48,1536]{2,1,0:T(8,128)(2,1)}, bf16[4,48,1536]{2,1,0:T(8,128)(2,1)}, u32[]{:S(2)}, u32[]{:S(2)}) collective-permute-start(bf16[4,48,1536]{2,1,0:T(8,128)(2,1)} %dynamic-slice_bitcast_fusion.7), channel_id=1, source_target_pairs={{0,8},{4,12},{8,0},{12,4},{1,9},{5,13},{9,1},{13,5},{2,10},{6,14},... | collective-permute-start | bytes 1769480 | tf_op jit(solution)/shard_map/ppermute | solution.py:770
  427.3 48.2 %collective-permute-start.101 = (bf16[4,48,1536]{2,1,0:T(8,128)(2,1)}, bf16[4,48,1536]{2,1,0:T(8,128)(2,1)}, u32[]{:S(2)}, u32[]{:S(2)}) collective-permute-start(bf16[4,48,1536]{2,1,0:T(8,128)(2,1)} %dynamic-slice_bitcast_fusion.6), channel_id=1, source_target_pairs={{0,8},{4,12},{8,0},{12,4},{1,9},{5,13},{9,1},{13,5},{2,10},{6,14},... | collective-permute-start | bytes 1769480 | tf_op jit(solution)/shard_map/ppermute | solution.py:770
  465.6 14.2 %collective-permute-start.97 = (bf16[48,1536]{1,0:T(8,128)(2,1)S(1)}, bf16[48,1536]{1,0:T(8,128)(2,1)S(1)}, u32[]{:S(2)}, u32[]{:S(2)}) collective-permute-start(bf16[48,1536]{1,0:T(8,128)(2,1)S(1)} %get-tuple-element.252), channel_id=1, source_target_pairs={{0,3},{1,2},{2,1},{3,0},{4,7},{5,6},{6,5},{7,4},{8,11},{9,10},{10,... | collective-permute-start | bytes 442376 | tf_op jit(solution)/shard_map/ppermute | solution.py:777
  477.5 22.6 %collective-permute-start.48 = (bf16[2,4,144,384]{3,2,1,0:T(8,128)(2,1)S(1)}, bf16[2,4,144,384]{3,2,1,0:T(8,128)(2,1)S(1)}, u32[]{:S(2)}, u32[]{:S(2)}) collective-permute-start(bf16[2,4,144,384]{3,2,1,0:T(8,128)(2,1)S(1)} %copy-done.42), channel_id=1, source_target_pairs={{0,8},{4,12},{8,0},{12,4},{1,9},{5,13},{9,1},{13,5},{2,10},{6,14},... | collective-permute-start | bytes 2654216 | tf_op jit(solution)/shard_map/ppermute | solution.py:770
  488.9 34.3 %collective-permute-start.78 = (bf16[2,4,192,384]{3,2,1,0:T(8,128)(2,1)S(1)}, bf16[2,4,192,384]{3,2,1,0:T(8,128)(2,1)S(1)}, u32[]{:S(2)}, u32[]{:S(2)}) collective-permute-start(bf16[2,4,192,384]{3,2,1,0:T(8,128)(2,1)S(1)} %copy-done.36), channel_id=1, source_target_pairs={{0,8},{4,12},{8,0},{12,4},{1,9},{5,13},{9,1},{13,5},{2,10},{6,14},... | collective-permute-start | bytes 3538952 | tf_op jit(solution)/shard_map/ppermute | solution.py:770
  489.9 14.4 %collective-permute-start.56 = (bf16[4,144,384]{2,1,0:T(8,128)(2,1)S(1)}, bf16[4,144,384]{2,1,0:T(8,128)(2,1)S(1)}, u32[]{:S(2)}, u32[]{:S(2)}) collective-permute-start(bf16[4,144,384]{2,1,0:T(8,128)(2,1)S(1)} %dynamic-slice_bitcast_fusion.10), channel_id=1, source_target_pairs={{0,4},{4,0},{8,12},{12,8},{1,5},{5,1},{9,13},{13,9},{2,6},{6,2},{1... | collective-permute-start | bytes 1327112 | tf_op jit(solution)/shard_map/ppermute | solution.py:770
  500.4 25.5 %collective-permute-start.49 = (bf16[4,144,384]{2,1,0:T(8,128)(2,1)S(1)}, bf16[4,144,384]{2,1,0:T(8,128)(2,1)S(1)}, u32[]{:S(2)}, u32[]{:S(2)}) collective-permute-start(bf16[4,144,384]{2,1,0:T(8,128)(2,1)S(1)} %dynamic-slice_bitcast_fusion.11), channel_id=1, source_target_pairs={{0,4},{4,0},{8,12},{12,8},{1,5},{5,1},{9,13},{13,9},{2,6},{6,2},{1... | collective-permute-start | bytes 1327112 | tf_op jit(solution)/shard_map/ppermute | solution.py:770
  503.3 24.0 %collective-permute-start.86 = (bf16[4,192,384]{2,1,0:T(8,128)(2,1)S(1)}, bf16[4,192,384]{2,1,0:T(8,128)(2,1)S(1)}, u32[]{:S(2)}, u32[]{:S(2)}) collective-permute-start(bf16[4,192,384]{2,1,0:T(8,128)(2,1)S(1)} %dynamic-slice_bitcast_fusion.8), channel_id=1, source_target_pairs={{0,4},{4,0},{8,12},{12,8},{1,5},{5,1},{9,13},{13,9},{2,6},{6,2},{1... | collective-permute-start | bytes 1769480 | tf_op jit(solution)/shard_map/ppermute | solution.py:770
  504.5 36.6 %collective-permute-start.57 = (bf16[144,384]{1,0:T(8,128)(2,1)S(1)}, bf16[144,384]{1,0:T(8,128)(2,1)S(1)}, u32[]{:S(2)}, u32[]{:S(2)}) collective-permute-start(bf16[144,384]{1,0:T(8,128)(2,1)S(1)} %get-tuple-element.260), channel_id=1, source_target_pairs={{0,1},{1,0},{2,3},{3,2},{4,5},{5,4},{6,7},{7,6},{8,9},{9,8},{10,11... | collective-permute-start | bytes 331784 | tf_op jit(solution)/shard_map/ppermute | solution.py:777
  507.9 35.0 %collective-permute-start.59 = (bf16[144,384]{1,0:T(8,128)(2,1)S(1)}, bf16[144,384]{1,0:T(8,128)(2,1)S(1)}, u32[]{:S(2)}, u32[]{:S(2)}) collective-permute-start(bf16[144,384]{1,0:T(8,128)(2,1)S(1)} %get-tuple-element.261), channel_id=1, source_target_pairs={{0,3},{1,2},{2,1},{3,0},{4,7},{5,6},{6,5},{7,4},{8,11},{9,10},{10,... | collective-permute-start | bytes 331784 | tf_op jit(solution)/shard_map/ppermute | solution.py:777
  523.2 19.8 %collective-permute-start.58 = (bf16[144,384]{1,0:T(8,128)(2,1)S(1)}, bf16[144,384]{1,0:T(8,128)(2,1)S(1)}, u32[]{:S(2)}, u32[]{:S(2)}) collective-permute-start(bf16[144,384]{1,0:T(8,128)(2,1)S(1)} %get-tuple-element.262), channel_id=1, source_target_pairs={{0,2},{1,3},{2,0},{3,1},{4,6},{5,7},{6,4},{7,5},{8,10},{9,11},{10,... | collective-permute-start | bytes 331784 | tf_op jit(solution)/shard_map/ppermute | solution.py:777
  527.3 17.8 %collective-permute-start.50 = (bf16[144,384]{1,0:T(8,128)(2,1)S(1)}, bf16[144,384]{1,0:T(8,128)(2,1)S(1)}, u32[]{:S(2)}, u32[]{:S(2)}) collective-permute-start(bf16[144,384]{1,0:T(8,128)(2,1)S(1)} %get-tuple-element.263), channel_id=1, source_target_pairs={{0,1},{1,0},{2,3},{3,2},{4,5},{5,4},{6,7},{7,6},{8,9},{9,8},{10,11... | collective-permute-start | bytes 331784 | tf_op jit(solution)/shard_map/ppermute | solution.py:777
  538.9 22.4 %collective-permute-start.87 = (bf16[192,384]{1,0:T(8,128)(2,1)S(1)}, bf16[192,384]{1,0:T(8,128)(2,1)S(1)}, u32[]{:S(2)}, u32[]{:S(2)}) collective-permute-start(bf16[192,384]{1,0:T(8,128)(2,1)S(1)} %get-tuple-element.254), channel_id=1, source_target_pairs={{0,1},{1,0},{2,3},{3,2},{4,5},{5,4},{6,7},{7,6},{8,9},{9,8},{10,11... | collective-permute-start | bytes 442376 | tf_op jit(solution)/shard_map/ppermute | solution.py:777
  542.9 16.5 %collective-permute-start.51 = (bf16[144,384]{1,0:T(8,128)(2,1)S(1)}, bf16[144,384]{1,0:T(8,128)(2,1)S(1)}, u32[]{:S(2)}, u32[]{:S(2)}) collective-permute-start(bf16[144,384]{1,0:T(8,128)(2,1)S(1)} %get-tuple-element.265), channel_id=1, source_target_pairs={{0,2},{1,3},{2,0},{3,1},{4,6},{5,7},{6,4},{7,5},{8,10},{9,11},{10,... | collective-permute-start | bytes 331784 | tf_op jit(solution)/shard_map/ppermute | solution.py:777
  543.0 18.4 %collective-permute-start.89 = (bf16[192,384]{1,0:T(8,128)(2,1)S(1)}, bf16[192,384]{1,0:T(8,128)(2,1)S(1)}, u32[]{:S(2)}, u32[]{:S(2)}) collective-permute-start(bf16[192,384]{1,0:T(8,128)(2,1)S(1)} %get-tuple-element.255), channel_id=1, source_target_pairs={{0,3},{1,2},{2,1},{3,0},{4,7},{5,6},{6,5},{7,4},{8,11},{9,10},{10,... | collective-permute-start | bytes 442376 | tf_op jit(solution)/shard_map/ppermute | solution.py:777
  545.0 27.0 %collective-permute-start.88 = (bf16[192,384]{1,0:T(8,128)(2,1)S(1)}, bf16[192,384]{1,0:T(8,128)(2,1)S(1)}, u32[]{:S(2)}, u32[]{:S(2)}) collective-permute-start(bf16[192,384]{1,0:T(8,128)(2,1)S(1)} %get-tuple-element.256), channel_id=1, source_target_pairs={{0,2},{1,3},{2,0},{3,1},{4,6},{5,7},{6,4},{7,5},{8,10},{9,11},{10,... | collective-permute-start | bytes 442376 | tf_op jit(solution)/shard_map/ppermute | solution.py:777
  549.7 22.3 %collective-permute-start.80 = (bf16[192,384]{1,0:T(8,128)(2,1)S(1)}, bf16[192,384]{1,0:T(8,128)(2,1)S(1)}, u32[]{:S(2)}, u32[]{:S(2)}) collective-permute-start(bf16[192,384]{1,0:T(8,128)(2,1)S(1)} %get-tuple-element.257), channel_id=1, source_target_pairs={{0,1},{1,0},{2,3},{3,2},{4,5},{5,4},{6,7},{7,6},{8,9},{9,8},{10,11... | collective-permute-start | bytes 442376 | tf_op jit(solution)/shard_map/ppermute | solution.py:777
  561.3 16.0 %collective-permute-start.81 = (bf16[192,384]{1,0:T(8,128)(2,1)S(1)}, bf16[192,384]{1,0:T(8,128)(2,1)S(1)}, u32[]{:S(2)}, u32[]{:S(2)}) collective-permute-start(bf16[192,384]{1,0:T(8,128)(2,1)S(1)} %get-tuple-element.259), channel_id=1, source_target_pairs={{0,2},{1,3},{2,0},{3,1},{4,6},{5,7},{6,4},{7,5},{8,10},{9,11},{10,... | collective-permute-start | bytes 442376 | tf_op jit(solution)/shard_map/ppermute | solution.py:777
  561.4 16.1 %collective-permute-start.60 = (f32[144,384]{1,0:T(8,128)S(1)}, f32[144,384]{1,0:T(8,128)S(1)}, u32[]{:S(2)}, u32[]{:S(2)}) collective-permute-start(f32[144,384]{1,0:T(8,128)S(1)} %get-tuple-element.217), channel_id=1, source_target_pairs={{0,16},{16,0},{1,17},{17,1},{2,18},{18,2},{3,19},{19,3},{4,20},{20... | collective-permute-start | bytes 663560 | tf_op jit(solution)/shard_map/ppermute | solution.py:741
  (165 other events, 1175.8 us)
